TPU v7x, 32 devices: a whole 2x2x4 slice. The times are simulated.
32 devices in a mesh: segment: 4 (over z), dp: 8 (over y, x, core).
Axes of the slice: x: 2, y: 2, z: 4, core: 2. Of those that a mesh axis runs over, the one named last changes fastest.
Arguments:
- images: bfloat16 [32, 16, 16, 256], P('dp'), may hold values from -6 to 6
- latent: float32 [32, 512], P('dp'), may hold values from -6 to 6
- weight: bfloat16 [4, 3, 3, 256, 256], P('segment'), may hold values from -0.125 to 0.125
- affine: float32 [4, 512, 256], P('segment'), may hold values from -0.25 to 0.25
- biases: float32 [4, 256], P('segment'), may hold values from -0.5 to 0.5
- cotangent: bfloat16 [32, 16, 16, 256], P('dp'), may hold values from -6 to 6
Outputs:
- grad_weight: float32 [4, 3, 3, 256, 256], P('segment')
- grad_affine: float32 [4, 512, 256], P('segment')
- grad_bias: float32 [4, 256], P('segment')
- grad_latent: float32 [32, 512], P('dp')
All inputs are finite; a program needn't handle non-finite values.
Results may differ from a plain program's by a relative error of at most 0.038.
Values may be sent and summed in bfloat16 or wider, within the bound.
A program may use at most 64 MiB of HBM per device.

v0:
```python
import math

import jax
import jax.numpy as jnp
from jax import lax
from jax.sharding import PartitionSpec as P

MICRO = 1
MB = 4


GAIN = math.sqrt(2.0)


def from_behind(value, axis, steps):
    count = lax.axis_size(axis)
    leading, last = (max(0, -steps), min(count, count - steps))
    return lax.ppermute(value, axis, [(source, source + steps) for source in range(leading, last)])


def synth_layer(inputs, latent_rows, kernel, affine_map, offsets):
    styles = jnp.dot(latent_rows, affine_map, precision=lax.Precision.HIGHEST) + 1.0
    energy = jnp.sum(jnp.square(kernel.astype(jnp.float32)), axis=(0, 1))
    demodulate = lax.rsqrt(
        jnp.dot(styles * styles, energy, precision=lax.Precision.HIGHEST) + 1e-08
    )
    scaled = (inputs.astype(jnp.float32) * styles[:, None, None, :]).astype(jnp.bfloat16)
    convolved = lax.conv_general_dilated(
        scaled,
        kernel,
        (1, 1),
        "SAME",
        dimension_numbers=("NHWC", "HWIO", "NHWC"),
        preferred_element_type=jnp.float32,
    )
    hidden = convolved * demodulate[:, None, None, :] + offsets
    return (GAIN * hidden * (0.6 + 0.4 * jnp.tanh(hidden))).astype(jnp.bfloat16)


def body(images, latent, weight, affine, biases, cotangent):
    kernel = weight[0]
    affine_map = affine[0]
    offsets = biases[0]
    segments = lax.axis_size("segment")
    segment_index = lax.axis_index("segment")
    ticks = MB + segments - 1
    map_shape = (MICRO,) + images.shape[1:]

    def forward_tick(tick, carry):
        incoming, saved = carry
        slot = tick - segment_index
        is_valid = (slot >= 0) & (slot < MB)
        clipped = jnp.clip(slot, 0, MB - 1)
        first_input = lax.dynamic_slice_in_dim(images, clipped * MICRO, MICRO, 0)
        inputs = jnp.where(segment_index == 0, first_input, incoming)
        latent_rows = lax.dynamic_slice_in_dim(latent, clipped * MICRO, MICRO, 0)
        result = synth_layer(inputs, latent_rows, kernel, affine_map, offsets)
        previous = lax.dynamic_index_in_dim(saved, clipped, 0, keepdims=False)
        saved = lax.dynamic_update_index_in_dim(
            saved, jnp.where(is_valid, inputs, previous), clipped, 0
        )
        incoming = from_behind(result, "segment", 1)
        return (incoming, saved)

    saved_start = jnp.zeros((MB,) + map_shape, jnp.bfloat16)
    incoming_start = jnp.zeros(map_shape, jnp.bfloat16)
    unused, saved = lax.fori_loop(0, ticks, forward_tick, (incoming_start, saved_start))
    weight_start = jnp.zeros(kernel.shape, jnp.float32)

    def backward_tick(tick, carry):
        arriving, weight_acc, affine_acc, bias_acc, latent_acc = carry
        slot = tick - (segments - 1 - segment_index)
        is_valid = (slot >= 0) & (slot < MB)
        clipped = jnp.clip(slot, 0, MB - 1)
        last_input = lax.dynamic_slice_in_dim(cotangent, clipped * MICRO, MICRO, 0)
        upstream = jnp.where(segment_index == segments - 1, last_input, arriving)
        inputs = lax.dynamic_index_in_dim(saved, clipped, 0, keepdims=False)
        latent_rows = lax.dynamic_slice_in_dim(latent, clipped * MICRO, MICRO, 0)
        result, pull = jax.vjp(synth_layer, inputs, latent_rows, kernel, affine_map, offsets)
        grad_input, part_latent, part_weight, part_affine, part_bias = pull(upstream)
        weight_term = jnp.where(is_valid, part_weight.astype(jnp.float32), 0.0)
        weight_acc = weight_acc + weight_term
        affine_acc = affine_acc + jnp.where(is_valid, part_affine, 0.0)
        bias_acc = bias_acc + jnp.where(is_valid, part_bias, 0.0)
        latent_old = lax.dynamic_slice_in_dim(latent_acc, clipped * MICRO, MICRO, 0)
        latent_new = jnp.where(is_valid, latent_old + part_latent, latent_old)
        latent_acc = lax.dynamic_update_slice_in_dim(latent_acc, latent_new, clipped * MICRO, 0)
        arriving = from_behind(grad_input, "segment", -1)
        return (arriving, weight_acc, affine_acc, bias_acc, latent_acc)

    start = (
        jnp.zeros(map_shape, jnp.bfloat16),
        weight_start,
        jnp.zeros(affine_map.shape, jnp.float32),
        jnp.zeros(offsets.shape, jnp.float32),
        jnp.zeros(latent.shape, jnp.float32),
    )
    unused, weight_acc, affine_acc, bias_acc, latent_acc = lax.fori_loop(
        0, ticks, backward_tick, start
    )
    weight_total, affine_total, bias_total = lax.psum((weight_acc, affine_acc, bias_acc), "dp")
    latent_total = lax.psum(latent_acc, "segment")
    return (weight_total[None], affine_total[None], bias_total[None], latent_total)


def solution(mesh):
    placed = (
        P("dp", None, None, None),
        P("dp", None),
        P("segment", None, None, None, None),
        P("segment", None, None),
        P("segment", None),
        P("dp", None, None, None),
    )
    return jax.shard_map(
        body,
        mesh=mesh,
        in_specs=placed,
        out_specs=(
            P("segment", None, None, None, None),
            P("segment", None, None),
            P("segment", None),
            P("dp", None),
        ),
        check_vma=False,
    )
```

profile of v0, /device:TPU:0, one launch (start us, length us, event | category | flops | bytes accessed | tf_op | source)
XLA Modules:
  0.0 327.1 jit_solution(10664480461018495916)
XLA Ops:
  7.2 1.5 multiply_reduce_fusion
  8.8 74.6 %while.41 = (s32[]{:T(128)}, bf16[1,16,16,256]{3,1,2,0:T(8,128)(2,1)S(1)}, bf16[4,1,16,16,256]{4,2,3,1,0:T(8,128)(2,1)S(1)}, pred[]{:T(512)}, s32[]{:T(128)}, /*...) while((s32[]{:T(128)}, ...), condition=%wide.region_2.3_spmd, body=%wide.region_1.2_spmd.sunk | while | flops 438633216 | bytes 11044319 | solution.py:67
  8.9 1.4 fusion.119
  12.5 4.9 %collective-permute-start = (bf16[1,16,16,256]{3,1,2,0:T(8,128)(2,1)S(1)}, bf16[1,16,16,256]{3,1,2,0:T(8,128)(2,1)S(1)}, u32[]{:S(2)}, u32[]{:S(2)}) collective-permute-start(bf16[1,16,16,256]{3,1,2,0:T(8,128)(2,1)S(1)} %slice_bitcast_fusion.9), channel_id=1, source_target_pairs={{0,8},{8,16},{16,24},{1,9},{9,17},{17,25},{2,10},{10,18},{18,26},{... | collective-permute-start | bytes 393224 | tf_op jit(solution)/shard_map/while/body/eval_jaxpr/ppermute | solution.py:18
  17.6 2.6 collective-permute-done
  23.9 4.4 %collective-permute-start = (bf16[1,16,16,256]{3,1,2,0:T(8,128)(2,1)S(1)}, bf16[1,16,16,256]{3,1,2,0:T(8,128)(2,1)S(1)}, u32[]{:S(2)}, u32[]{:S(2)}) collective-permute-start(bf16[1,16,16,256]{3,1,2,0:T(8,128)(2,1)S(1)} %slice_bitcast_fusion.9), channel_id=1, source_target_pairs={{0,8},{8,16},{16,24},{1,9},{9,17},{17,25},{2,10},{10,18},{18,26},{... | collective-permute-start | bytes 393224 | tf_op jit(solution)/shard_map/while/body/eval_jaxpr/ppermute | solution.py:18
  28.4 2.4 collective-permute-done
  30.8 1.4 fusion.119
  34.4 4.4 %collective-permute-start = (bf16[1,16,16,256]{3,1,2,0:T(8,128)(2,1)S(1)}, bf16[1,16,16,256]{3,1,2,0:T(8,128)(2,1)S(1)}, u32[]{:S(2)}, u32[]{:S(2)}) collective-permute-start(bf16[1,16,16,256]{3,1,2,0:T(8,128)(2,1)S(1)} %slice_bitcast_fusion.9), channel_id=1, source_target_pairs={{0,8},{8,16},{16,24},{1,9},{9,17},{17,25},{2,10},{10,18},{18,26},{... | collective-permute-start | bytes 393224 | tf_op jit(solution)/shard_map/while/body/eval_jaxpr/ppermute | solution.py:18
  38.9 2.4 collective-permute-done
  45.0 4.4 %collective-permute-start = (bf16[1,16,16,256]{3,1,2,0:T(8,128)(2,1)S(1)}, bf16[1,16,16,256]{3,1,2,0:T(8,128)(2,1)S(1)}, u32[]{:S(2)}, u32[]{:S(2)}) collective-permute-start(bf16[1,16,16,256]{3,1,2,0:T(8,128)(2,1)S(1)} %slice_bitcast_fusion.9), channel_id=1, source_target_pairs={{0,8},{8,16},{16,24},{1,9},{9,17},{17,25},{2,10},{10,18},{18,26},{... | collective-permute-start | bytes 393224 | tf_op jit(solution)/shard_map/while/body/eval_jaxpr/ppermute | solution.py:18
  49.4 2.4 collective-permute-done
  55.5 4.4 %collective-permute-start = (bf16[1,16,16,256]{3,1,2,0:T(8,128)(2,1)S(1)}, bf16[1,16,16,256]{3,1,2,0:T(8,128)(2,1)S(1)}, u32[]{:S(2)}, u32[]{:S(2)}) collective-permute-start(bf16[1,16,16,256]{3,1,2,0:T(8,128)(2,1)S(1)} %slice_bitcast_fusion.9), channel_id=1, source_target_pairs={{0,8},{8,16},{16,24},{1,9},{9,17},{17,25},{2,10},{10,18},{18,26},{... | collective-permute-start | bytes 393224 | tf_op jit(solution)/shard_map/while/body/eval_jaxpr/ppermute | solution.py:18
  60.0 2.4 collective-permute-done
  62.4 1.4 fusion.119
  66.0 4.4 %collective-permute-start = (bf16[1,16,16,256]{3,1,2,0:T(8,128)(2,1)S(1)}, bf16[1,16,16,256]{3,1,2,0:T(8,128)(2,1)S(1)}, u32[]{:S(2)}, u32[]{:S(2)}) collective-permute-start(bf16[1,16,16,256]{3,1,2,0:T(8,128)(2,1)S(1)} %slice_bitcast_fusion.9), channel_id=1, source_target_pairs={{0,8},{8,16},{16,24},{1,9},{9,17},{17,25},{2,10},{10,18},{18,26},{... | collective-permute-start | bytes 393224 | tf_op jit(solution)/shard_map/while/body/eval_jaxpr/ppermute | solution.py:18
  70.5 2.4 collective-permute-done
  73.0 1.4 fusion.119
  76.6 4.4 %collective-permute-start = (bf16[1,16,16,256]{3,1,2,0:T(8,128)(2,1)S(1)}, bf16[1,16,16,256]{3,1,2,0:T(8,128)(2,1)S(1)}, u32[]{:S(2)}, u32[]{:S(2)}) collective-permute-start(bf16[1,16,16,256]{3,1,2,0:T(8,128)(2,1)S(1)} %slice_bitcast_fusion.9), channel_id=1, source_target_pairs={{0,8},{8,16},{16,24},{1,9},{9,17},{17,25},{2,10},{10,18},{18,26},{... | collective-permute-start | bytes 393224 | tf_op jit(solution)/shard_map/while/body/eval_jaxpr/ppermute | solution.py:18
  81.0 2.4 collective-permute-done
  84.1 156.6 %while.42 = (s32[]{:T(128)}, bf16[1,16,16,256]{3,1,2,0:T(8,128)(2,1)S(1)}, f32[3,3,256,256]{3,2,1,0:T(8,128)}, f32[512,256]{1,0:T(8,128)S(1)}, f32[256]{0:T(256)...) while((s32[]{:T(128)}, ...), condition=%wide.region_8.9_spmd.clone, body=%wide.region_3.8_spmd.clone.sunk | while | flops 1162186496 | bytes 33860464 | solution.py:98
  101.1 3.4 %select_add_fusion.6 = f32[3,3,256,256]{3,2,1,0:T(8,128)} fusion(f32[3,3,256,256]{3,2,1,0:T(8,128)} %get-tuple-element.953, pred[]{:T(512)S(6)} %compare.35, pred[]{:T(512)S(6)} %and.23, f32[256,256]{1,0:T(8,128)S(1)} %multiply_multiply_fusion.5, bf16[3,3,256,256]{3,2,1,0:T(8,128)(2,1)S(1)} %copy-done.2, ...), kind=kOutput, calls=%fused_computation.34.clone.1 | convolution fusion | flops 282066944 | bytes 6422530 | tf_op jit(solution)/shard_map/while/body/eval_jaxpr/transpose(jvp())/conv_general_dilated | solution.py:28
  122.0 5.1 %select_add_fusion.6 = f32[3,3,256,256]{3,2,1,0:T(8,128)} fusion(f32[3,3,256,256]{3,2,1,0:T(8,128)} %get-tuple-element.953, pred[]{:T(512)S(6)} %compare.35, pred[]{:T(512)S(6)} %and.23, f32[256,256]{1,0:T(8,128)S(1)} %multiply_multiply_fusion.5, bf16[3,3,256,256]{3,2,1,0:T(8,128)(2,1)S(1)} %copy-done.2, ...), kind=kOutput, calls=%fused_computation.34.clone.1 | convolution fusion | flops 282066944 | bytes 6422530 | tf_op jit(solution)/shard_map/while/body/eval_jaxpr/transpose(jvp())/conv_general_dilated | solution.py:28
  144.6 5.1 %select_add_fusion.6 = f32[3,3,256,256]{3,2,1,0:T(8,128)} fusion(f32[3,3,256,256]{3,2,1,0:T(8,128)} %get-tuple-element.953, pred[]{:T(512)S(6)} %compare.35, pred[]{:T(512)S(6)} %and.23, f32[256,256]{1,0:T(8,128)S(1)} %multiply_multiply_fusion.5, bf16[3,3,256,256]{3,2,1,0:T(8,128)(2,1)S(1)} %copy-done.2, ...), kind=kOutput, calls=%fused_computation.34.clone.1 | convolution fusion | flops 282066944 | bytes 6422530 | tf_op jit(solution)/shard_map/while/body/eval_jaxpr/transpose(jvp())/conv_general_dilated | solution.py:28
  167.2 5.1 %select_add_fusion.6 = f32[3,3,256,256]{3,2,1,0:T(8,128)} fusion(f32[3,3,256,256]{3,2,1,0:T(8,128)} %get-tuple-element.953, pred[]{:T(512)S(6)} %compare.35, pred[]{:T(512)S(6)} %and.23, f32[256,256]{1,0:T(8,128)S(1)} %multiply_multiply_fusion.5, bf16[3,3,256,256]{3,2,1,0:T(8,128)(2,1)S(1)} %copy-done.2, ...), kind=kOutput, calls=%fused_computation.34.clone.1 | convolution fusion | flops 282066944 | bytes 6422530 | tf_op jit(solution)/shard_map/while/body/eval_jaxpr/transpose(jvp())/conv_general_dilated | solution.py:28
  189.8 5.1 %select_add_fusion.6 = f32[3,3,256,256]{3,2,1,0:T(8,128)} fusion(f32[3,3,256,256]{3,2,1,0:T(8,128)} %get-tuple-element.953, pred[]{:T(512)S(6)} %compare.35, pred[]{:T(512)S(6)} %and.23, f32[256,256]{1,0:T(8,128)S(1)} %multiply_multiply_fusion.5, bf16[3,3,256,256]{3,2,1,0:T(8,128)(2,1)S(1)} %copy-done.2, ...), kind=kOutput, calls=%fused_computation.34.clone.1 | convolution fusion | flops 282066944 | bytes 6422530 | tf_op jit(solution)/shard_map/while/body/eval_jaxpr/transpose(jvp())/conv_general_dilated | solution.py:28
  212.4 5.1 %select_add_fusion.6 = f32[3,3,256,256]{3,2,1,0:T(8,128)} fusion(f32[3,3,256,256]{3,2,1,0:T(8,128)} %get-tuple-element.953, pred[]{:T(512)S(6)} %compare.35, pred[]{:T(512)S(6)} %and.23, f32[256,256]{1,0:T(8,128)S(1)} %multiply_multiply_fusion.5, bf16[3,3,256,256]{3,2,1,0:T(8,128)(2,1)S(1)} %copy-done.2, ...), kind=kOutput, calls=%fused_computation.34.clone.1 | convolution fusion | flops 282066944 | bytes 6422530 | tf_op jit(solution)/shard_map/while/body/eval_jaxpr/transpose(jvp())/conv_general_dilated | solution.py:28
  235.0 5.1 %select_add_fusion.6 = f32[3,3,256,256]{3,2,1,0:T(8,128)} fusion(f32[3,3,256,256]{3,2,1,0:T(8,128)} %get-tuple-element.953, pred[]{:T(512)S(6)} %compare.35, pred[]{:T(512)S(6)} %and.23, f32[256,256]{1,0:T(8,128)S(1)} %multiply_multiply_fusion.5, bf16[3,3,256,256]{3,2,1,0:T(8,128)(2,1)S(1)} %copy-done.2, ...), kind=kOutput, calls=%fused_computation.34.clone.1 | convolution fusion | flops 282066944 | bytes 6422530 | tf_op jit(solution)/shard_map/while/body/eval_jaxpr/transpose(jvp())/conv_general_dilated | solution.py:28
  241.5 12.4 %psum.30 = f32[1,256]{1,0:T(1,128)} all-reduce(f32[1,256]{1,0:T(1,128)S(1)} %bitcast.237), channel_id=1, replica_groups=mesh['segment'=4,'dp'=8] {'dp'}, use_global_device_ids=true, to_apply=%region_11.12 | all-reduce | flops 256 | bytes 2048 | tf_op jit(solution)/shard_map/psum | solution.py:101
  253.9 18.9 %psum.31 = f32[4,512]{1,0:T(4,128)} all-reduce(f32[4,512]{1,0:T(4,128)S(1)} %copy-done.9), channel_id=1, replica_groups=mesh['segment'=4,'dp'=8] {'segment'}, use_global_device_ids=true, to_apply=%region_12.13 | all-reduce | flops 2048 | bytes 16384 | tf_op jit(solution)/shard_map/psum | solution.py:102
  272.8 43.4 %all-reduce.3.cloned.1.call-done = (f32[1,3,3,256,256]{4,3,2,1,0:T(8,128)}, f32[1,512,256]{2,1,0:T(8,128)}) async-done(((f32[1,3,3,256,256]{4,3,2,1,0:T(8,128)}, f32[1,512,256]{2,1,0:T(8,128)}), (f32[1,3,3,256,256]{4,3,2,1,0:T(8,128)}, f32[1,512,256]{2,1,0:T(8,128)})) %all-reduce.3.cloned.1.call-update) | async-done | bytes 2883600 | tf_op jit(solution)/shard_map/psum | solution.py:101
  316.2 3.3 %copy.106 = f32[1,3,3,256,256]{4,3,2,1,0:T(8,128)} copy(f32[1,3,3,256,256]{4,3,2,1,0:T(8,128)} %get-tuple-element.993) | data formatting | bytes 4718592
  (581 shorter events, 142.9 us)
Async XLA Ops:
  7.2 309.0 %all-reduce.3.cloned.1.call-start = ((), (), s32[]{:S(2)}) async-start(), calls=%async_computation | async-start | bytes 5767168 | tf_op jit(solution)/shard_map/psum | solution.py:101
  12.5 7.7 %collective-permute-start = (bf16[1,16,16,256]{3,1,2,0:T(8,128)(2,1)S(1)}, bf16[1,16,16,256]{3,1,2,0:T(8,128)(2,1)S(1)}, u32[]{:S(2)}, u32[]{:S(2)}) collective-permute-start(bf16[1,16,16,256]{3,1,2,0:T(8,128)(2,1)S(1)} %slice_bitcast_fusion.9), channel_id=1, source_target_pairs={{0,8},{8,16},{16,24},{1,9},{9,17},{17,25},{2,10},{10,18},{18,26},{... | collective-permute-start | bytes 393224 | tf_op jit(solution)/shard_map/while/body/eval_jaxpr/ppermute | solution.py:18
  23.9 6.9 %collective-permute-start = (bf16[1,16,16,256]{3,1,2,0:T(8,128)(2,1)S(1)}, bf16[1,16,16,256]{3,1,2,0:T(8,128)(2,1)S(1)}, u32[]{:S(2)}, u32[]{:S(2)}) collective-permute-start(bf16[1,16,16,256]{3,1,2,0:T(8,128)(2,1)S(1)} %slice_bitcast_fusion.9), channel_id=1, source_target_pairs={{0,8},{8,16},{16,24},{1,9},{9,17},{17,25},{2,10},{10,18},{18,26},{... | collective-permute-start | bytes 393224 | tf_op jit(solution)/shard_map/while/body/eval_jaxpr/ppermute | solution.py:18
  34.4 6.9 %collective-permute-start = (bf16[1,16,16,256]{3,1,2,0:T(8,128)(2,1)S(1)}, bf16[1,16,16,256]{3,1,2,0:T(8,128)(2,1)S(1)}, u32[]{:S(2)}, u32[]{:S(2)}) collective-permute-start(bf16[1,16,16,256]{3,1,2,0:T(8,128)(2,1)S(1)} %slice_bitcast_fusion.9), channel_id=1, source_target_pairs={{0,8},{8,16},{16,24},{1,9},{9,17},{17,25},{2,10},{10,18},{18,26},{... | collective-permute-start | bytes 393224 | tf_op jit(solution)/shard_map/while/body/eval_jaxpr/ppermute | solution.py:18
  45.0 6.9 %collective-permute-start = (bf16[1,16,16,256]{3,1,2,0:T(8,128)(2,1)S(1)}, bf16[1,16,16,256]{3,1,2,0:T(8,128)(2,1)S(1)}, u32[]{:S(2)}, u32[]{:S(2)}) collective-permute-start(bf16[1,16,16,256]{3,1,2,0:T(8,128)(2,1)S(1)} %slice_bitcast_fusion.9), channel_id=1, source_target_pairs={{0,8},{8,16},{16,24},{1,9},{9,17},{17,25},{2,10},{10,18},{18,26},{... | collective-permute-start | bytes 393224 | tf_op jit(solution)/shard_map/while/body/eval_jaxpr/ppermute | solution.py:18
  55.5 6.9 %collective-permute-start = (bf16[1,16,16,256]{3,1,2,0:T(8,128)(2,1)S(1)}, bf16[1,16,16,256]{3,1,2,0:T(8,128)(2,1)S(1)}, u32[]{:S(2)}, u32[]{:S(2)}) collective-permute-start(bf16[1,16,16,256]{3,1,2,0:T(8,128)(2,1)S(1)} %slice_bitcast_fusion.9), channel_id=1, source_target_pairs={{0,8},{8,16},{16,24},{1,9},{9,17},{17,25},{2,10},{10,18},{18,26},{... | collective-permute-start | bytes 393224 | tf_op jit(solution)/shard_map/while/body/eval_jaxpr/ppermute | solution.py:18
  66.0 6.9 %collective-permute-start = (bf16[1,16,16,256]{3,1,2,0:T(8,128)(2,1)S(1)}, bf16[1,16,16,256]{3,1,2,0:T(8,128)(2,1)S(1)}, u32[]{:S(2)}, u32[]{:S(2)}) collective-permute-start(bf16[1,16,16,256]{3,1,2,0:T(8,128)(2,1)S(1)} %slice_bitcast_fusion.9), channel_id=1, source_target_pairs={{0,8},{8,16},{16,24},{1,9},{9,17},{17,25},{2,10},{10,18},{18,26},{... | collective-permute-start | bytes 393224 | tf_op jit(solution)/shard_map/while/body/eval_jaxpr/ppermute | solution.py:18
  76.6 6.9 %collective-permute-start = (bf16[1,16,16,256]{3,1,2,0:T(8,128)(2,1)S(1)}, bf16[1,16,16,256]{3,1,2,0:T(8,128)(2,1)S(1)}, u32[]{:S(2)}, u32[]{:S(2)}) collective-permute-start(bf16[1,16,16,256]{3,1,2,0:T(8,128)(2,1)S(1)} %slice_bitcast_fusion.9), channel_id=1, source_target_pairs={{0,8},{8,16},{16,24},{1,9},{9,17},{17,25},{2,10},{10,18},{18,26},{... | collective-permute-start | bytes 393224 | tf_op jit(solution)/shard_map/while/body/eval_jaxpr/ppermute | solution.py:18
  91.2 7.1 %copy-start = (f32[512,256]{1,0:T(8,128)S(1)}, f32[512,256]{1,0:T(8,128)}, u32[]{:S(2)}) copy-start(f32[512,256]{1,0:T(8,128)} %get-tuple-element.981) | copy-start | bytes 1572868 | tf_op jit(solution)/shard_map/while
  93.3 11.2 %collective-permute-start.1 = (bf16[1,16,16,256]{3,1,2,0:T(8,128)(2,1)}, bf16[1,16,16,256]{3,1,2,0:T(8,128)(2,1)S(1)}, u32[]{:S(2)}, u32[]{:S(2)}) collective-permute-start(bf16[1,16,16,256]{3,1,2,0:T(8,128)(2,1)} %slice_bitcast_fusion.10), channel_id=1, source_target_pairs={{8,0},{16,8},{24,16},{9,1},{17,9},{25,17},{10,2},{18,10},{26,18},{... | collective-permute-start | bytes 393224 | tf_op jit(solution)/shard_map/while/body/eval_jaxpr/ppermute | solution.py:18
  112.1 7.1 %copy-start = (f32[512,256]{1,0:T(8,128)S(1)}, f32[512,256]{1,0:T(8,128)}, u32[]{:S(2)}) copy-start(f32[512,256]{1,0:T(8,128)} %get-tuple-element.981) | copy-start | bytes 1572868 | tf_op jit(solution)/shard_map/while
  114.2 12.9 %collective-permute-start.1 = (bf16[1,16,16,256]{3,1,2,0:T(8,128)(2,1)}, bf16[1,16,16,256]{3,1,2,0:T(8,128)(2,1)S(1)}, u32[]{:S(2)}, u32[]{:S(2)}) collective-permute-start(bf16[1,16,16,256]{3,1,2,0:T(8,128)(2,1)} %slice_bitcast_fusion.10), channel_id=1, source_target_pairs={{8,0},{16,8},{24,16},{9,1},{17,9},{25,17},{10,2},{18,10},{26,18},{... | collective-permute-start | bytes 393224 | tf_op jit(solution)/shard_map/while/body/eval_jaxpr/ppermute | solution.py:18
  122.0 5.1 %copy-start.8 = (f32[256]{0:T(256)S(1)}, f32[256]{0:T(256)}, u32[]{:S(2)}) copy-start(f32[256]{0:T(256)} %get-tuple-element.878) | copy-start | bytes 3076 | tf_op jit(solution)/shard_map/while
  122.0 5.1 %copy-start.10 = (f32[256]{0:T(256)S(1)}, f32[256]{0:T(256)}, u32[]{:S(2)}) copy-start(f32[256]{0:T(256)} %get-tuple-element.955) | copy-start | bytes 3076 | tf_op jit(solution)/shard_map/while
  134.7 7.1 %copy-start = (f32[512,256]{1,0:T(8,128)S(1)}, f32[512,256]{1,0:T(8,128)}, u32[]{:S(2)}) copy-start(f32[512,256]{1,0:T(8,128)} %get-tuple-element.981) | copy-start | bytes 1572868 | tf_op jit(solution)/shard_map/while
  136.8 12.9 %collective-permute-start.1 = (bf16[1,16,16,256]{3,1,2,0:T(8,128)(2,1)}, bf16[1,16,16,256]{3,1,2,0:T(8,128)(2,1)S(1)}, u32[]{:S(2)}, u32[]{:S(2)}) collective-permute-start(bf16[1,16,16,256]{3,1,2,0:T(8,128)(2,1)} %slice_bitcast_fusion.10), channel_id=1, source_target_pairs={{8,0},{16,8},{24,16},{9,1},{17,9},{25,17},{10,2},{18,10},{26,18},{... | collective-permute-start | bytes 393224 | tf_op jit(solution)/shard_map/while/body/eval_jaxpr/ppermute | solution.py:18
  144.6 5.1 %copy-start.8 = (f32[256]{0:T(256)S(1)}, f32[256]{0:T(256)}, u32[]{:S(2)}) copy-start(f32[256]{0:T(256)} %get-tuple-element.878) | copy-start | bytes 3076 | tf_op jit(solution)/shard_map/while
  144.6 5.1 %copy-start.10 = (f32[256]{0:T(256)S(1)}, f32[256]{0:T(256)}, u32[]{:S(2)}) copy-start(f32[256]{0:T(256)} %get-tuple-element.955) | copy-start | bytes 3076 | tf_op jit(solution)/shard_map/while
  157.3 7.1 %copy-start = (f32[512,256]{1,0:T(8,128)S(1)}, f32[512,256]{1,0:T(8,128)}, u32[]{:S(2)}) copy-start(f32[512,256]{1,0:T(8,128)} %get-tuple-element.981) | copy-start | bytes 1572868 | tf_op jit(solution)/shard_map/while
  159.4 12.9 %collective-permute-start.1 = (bf16[1,16,16,256]{3,1,2,0:T(8,128)(2,1)}, bf16[1,16,16,256]{3,1,2,0:T(8,128)(2,1)S(1)}, u32[]{:S(2)}, u32[]{:S(2)}) collective-permute-start(bf16[1,16,16,256]{3,1,2,0:T(8,128)(2,1)} %slice_bitcast_fusion.10), channel_id=1, source_target_pairs={{8,0},{16,8},{24,16},{9,1},{17,9},{25,17},{10,2},{18,10},{26,18},{... | collective-permute-start | bytes 393224 | tf_op jit(solution)/shard_map/while/body/eval_jaxpr/ppermute | solution.py:18
  167.2 5.1 %copy-start.8 = (f32[256]{0:T(256)S(1)}, f32[256]{0:T(256)}, u32[]{:S(2)}) copy-start(f32[256]{0:T(256)} %get-tuple-element.878) | copy-start | bytes 3076 | tf_op jit(solution)/shard_map/while
  167.2 5.1 %copy-start.10 = (f32[256]{0:T(256)S(1)}, f32[256]{0:T(256)}, u32[]{:S(2)}) copy-start(f32[256]{0:T(256)} %get-tuple-element.955) | copy-start | bytes 3076 | tf_op jit(solution)/shard_map/while
  179.9 7.1 %copy-start = (f32[512,256]{1,0:T(8,128)S(1)}, f32[512,256]{1,0:T(8,128)}, u32[]{:S(2)}) copy-start(f32[512,256]{1,0:T(8,128)} %get-tuple-element.981) | copy-start | bytes 1572868 | tf_op jit(solution)/shard_map/while
  182.1 12.9 %collective-permute-start.1 = (bf16[1,16,16,256]{3,1,2,0:T(8,128)(2,1)}, bf16[1,16,16,256]{3,1,2,0:T(8,128)(2,1)S(1)}, u32[]{:S(2)}, u32[]{:S(2)}) collective-permute-start(bf16[1,16,16,256]{3,1,2,0:T(8,128)(2,1)} %slice_bitcast_fusion.10), channel_id=1, source_target_pairs={{8,0},{16,8},{24,16},{9,1},{17,9},{25,17},{10,2},{18,10},{26,18},{... | collective-permute-start | bytes 393224 | tf_op jit(solution)/shard_map/while/body/eval_jaxpr/ppermute | solution.py:18
  189.8 5.1 %copy-start.8 = (f32[256]{0:T(256)S(1)}, f32[256]{0:T(256)}, u32[]{:S(2)}) copy-start(f32[256]{0:T(256)} %get-tuple-element.878) | copy-start | bytes 3076 | tf_op jit(solution)/shard_map/while
  202.5 7.1 %copy-start = (f32[512,256]{1,0:T(8,128)S(1)}, f32[512,256]{1,0:T(8,128)}, u32[]{:S(2)}) copy-start(f32[512,256]{1,0:T(8,128)} %get-tuple-element.981) | copy-start | bytes 1572868 | tf_op jit(solution)/shard_map/while
  204.7 12.9 %collective-permute-start.1 = (bf16[1,16,16,256]{3,1,2,0:T(8,128)(2,1)}, bf16[1,16,16,256]{3,1,2,0:T(8,128)(2,1)S(1)}, u32[]{:S(2)}, u32[]{:S(2)}) collective-permute-start(bf16[1,16,16,256]{3,1,2,0:T(8,128)(2,1)} %slice_bitcast_fusion.10), channel_id=1, source_target_pairs={{8,0},{16,8},{24,16},{9,1},{17,9},{25,17},{10,2},{18,10},{26,18},{... | collective-permute-start | bytes 393224 | tf_op jit(solution)/shard_map/while/body/eval_jaxpr/ppermute | solution.py:18
  212.4 5.1 %copy-start.8 = (f32[256]{0:T(256)S(1)}, f32[256]{0:T(256)}, u32[]{:S(2)}) copy-start(f32[256]{0:T(256)} %get-tuple-element.878) | copy-start | bytes 3076 | tf_op jit(solution)/shard_map/while
  225.1 7.1 %copy-start = (f32[512,256]{1,0:T(8,128)S(1)}, f32[512,256]{1,0:T(8,128)}, u32[]{:S(2)}) copy-start(f32[512,256]{1,0:T(8,128)} %get-tuple-element.981) | copy-start | bytes 1572868 | tf_op jit(solution)/shard_map/while
  227.3 12.9 %collective-permute-start.1 = (bf16[1,16,16,256]{3,1,2,0:T(8,128)(2,1)}, bf16[1,16,16,256]{3,1,2,0:T(8,128)(2,1)S(1)}, u32[]{:S(2)}, u32[]{:S(2)}) collective-permute-start(bf16[1,16,16,256]{3,1,2,0:T(8,128)(2,1)} %slice_bitcast_fusion.10), channel_id=1, source_target_pairs={{8,0},{16,8},{24,16},{9,1},{17,9},{25,17},{10,2},{18,10},{26,18},{... | collective-permute-start | bytes 393224 | tf_op jit(solution)/shard_map/while/body/eval_jaxpr/ppermute | solution.py:18
  235.0 5.1 %copy-start.8 = (f32[256]{0:T(256)S(1)}, f32[256]{0:T(256)}, u32[]{:S(2)}) copy-start(f32[256]{0:T(256)} %get-tuple-element.878) | copy-start | bytes 3076 | tf_op jit(solution)/shard_map/while
  240.7 13.2 %copy-start.9 = (f32[4,512]{1,0:T(4,128)S(1)}, f32[4,512]{1,0:T(4,128)}, u32[]{:S(2)}) copy-start(f32[4,512]{1,0:T(4,128)} %get-tuple-element.551) | copy-start | bytes 24580
  (85 other events, 236.0 us)
Sparse Core Ops, SparseCore 0:
  241.6 74.5 all-reduce.2
where the time goes:
time: 329 us; the launch traced here: 327 us
  matrix products  85 us (26%)
  local copies, waits for them, and re-layouts  65.3 us (20%)
  waiting for transfers between devices  60.3 us (18%)
  starting transfers between devices  40.1 us (12%)
  blocking collectives  31.3 us (10%)
  other arithmetic  27.8 us (8%)
  between operations  14.1 us (4%)
    conv_general_dilated x28, matrix products, synth_layer(): lax.conv_general_dilated(scaled, kernel, (1, 1), 'SAME', dimension_number...  53 us
    psum x1, waiting for transfers between devices, body(): lax.psum((weight_acc, affine_acc, bias_acc), 'dp')  43.4 us
    ppermute x14, starting transfers between devices, from_behind(): lax.ppermute(value, axis, [(source, source + steps) for source in range(l...  40.1 us
    dot_general x21, matrix products, synth_layer(): jnp.dot(latent_rows, affine_map, precision=lax.Precision.HIGHEST) + 1.0  27.6 us
    psum x1, blocking collectives, body(): latent_total = lax.psum(latent_acc, 'segment')  18.9 us
    ppermute x14, waiting for transfers between devices, from_behind(): lax.ppermute(value, axis, [(source, source + steps) for source in range(l...  16.9 us
    psum x1, blocking collectives, body(): lax.psum((weight_acc, affine_acc, bias_acc), 'dp')  12.4 us
    while x203, local copies, waits for them, and re-layouts  12 us
  transfers between devices with their start and end apart: 15, of which 8 were waited for; matrix products, arithmetic and copies ran while one was open for 24% of the time, Pallas kernels for 0%

commit v1 on v0

v1 whole, which is shorter than its diff:
```python
import functools
import math

import jax
import jax.numpy as jnp
from jax import lax
from jax.experimental import pallas as pl
from jax.experimental.pallas import tpu as pltpu
from jax.sharding import PartitionSpec as P

GAIN = math.sqrt(2.0)
MESH = pl.DeviceIdType.MESH
F32 = jnp.float32
BF16 = jnp.bfloat16
NN = (((1,), (0,)), ((), ()))
NT = (((1,), (1,)), ((), ()))
TN = (((0,), (0,)), ((), ()))


def exact(a, b, dims):
    return lax.dot_general(
        a, b, dims, precision=lax.Precision.HIGHEST, preferred_element_type=F32
    )


def relay(
    segments, width,
    images, latent, weight, affine, biases, cotangent,
    wgrad_out, rows_out, latent_out,
    fin, fout, gin, gout, spread_x, conv, slope, flipped, spread_g, acc, energy,
    styles, demod, d_demod, d_style, d_bias,
    f_send, f_recv, g_send, g_recv,
):
    count, pixels, chans = images.shape
    seg = lax.axis_index("segment")
    first, last = seg == 0, seg == segments - 1
    up, down = jnp.minimum(seg + 1, segments - 1), jnp.maximum(seg - 1, 0)

    barrier = pltpu.get_barrier_semaphore()

    @pl.when(jnp.logical_not(first))
    def _():
        pl.semaphore_signal(barrier, inc=1, device_id={"segment": down}, device_id_type=MESH)

    @pl.when(jnp.logical_not(last))
    def _():
        pl.semaphore_signal(barrier, inc=1, device_id={"segment": up}, device_id_type=MESH)

    pl.semaphore_wait(barrier, jnp.where(first, 0, 1) + jnp.where(last, 0, 1))

    def forward_copy(n):
        return pltpu.make_async_remote_copy(
            src_ref=fout.at[n], dst_ref=fin.at[n], send_sem=f_send.at[n],
            recv_sem=f_recv.at[n], device_id={"segment": up}, device_id_type=MESH,
        )

    def backward_copy(n):
        return pltpu.make_async_remote_copy(
            src_ref=gout.at[n], dst_ref=gin.at[n], send_sem=g_send.at[n],
            recv_sem=g_recv.at[n], device_id={"segment": down}, device_id_type=MESH,
        )

    column = lax.rem(lax.broadcasted_iota(jnp.int32, (pixels, chans), 0), width)
    at_left, at_right = column == 0, column == width - 1

    def spread(target, value):
        body = slice(width, width + pixels)
        target[body, chans:2 * chans] = value.astype(BF16)
        target[body, :chans] = jnp.where(at_left, 0.0, pltpu.roll(value, 1, 0)).astype(BF16)
        target[body, 2 * chans:] = jnp.where(
            at_right, 0.0, pltpu.roll(value, pixels - 1, 0)
        ).astype(BF16)

    def conv3(source, kernel):
        total = jnp.dot(source[0:pixels, :], kernel[0], preferred_element_type=F32)
        for dy in (1, 2):
            total += jnp.dot(
                source[dy * width:dy * width + pixels, :], kernel[dy], preferred_element_type=F32
            )
        return total

    total = jnp.zeros((chans, chans), F32)
    for dy in range(3):
        for dx in range(3):
            total += jnp.square(weight[dy, dx * chans:(dx + 1) * chans, :].astype(F32))
    energy[...] = total
    style_rows = exact(latent[...], affine[...], NN) + 1.0
    demod_rows = lax.rsqrt(exact(style_rows * style_rows, total, NN) + 1e-08)
    edge = jnp.zeros((width, 3 * chans), BF16)
    for n in range(count):
        styles[n] = style_rows[n:n + 1, :]
        demod[n] = demod_rows[n:n + 1, :]
        spread_x[n, 0:width, :] = edge
        spread_x[n, width + pixels:, :] = edge
    spread_g[0:width, :] = edge
    spread_g[width + pixels:, :] = edge

    def forward(n, carry):
        @pl.when(first)
        def _():
            fin[n] = images[n]

        @pl.when(jnp.logical_not(first))
        def _():
            forward_copy(n).wait_recv()

        spread(spread_x.at[n], fin[n].astype(F32) * styles[n])
        convolved = conv3(spread_x.at[n], weight)
        conv[n] = convolved
        hidden = convolved * demod[n] + biases[...]
        gate = jnp.tanh(hidden)
        fout[n] = (GAIN * hidden * (0.6 + 0.4 * gate)).astype(BF16)

        @pl.when(jnp.logical_not(last))
        def _():
            forward_copy(n).start()

        slope[n] = GAIN * (0.6 + 0.4 * gate + 0.4 * hidden * (1.0 - gate * gate))
        return carry

    lax.fori_loop(0, count, forward, 0)

    for dy in range(3):
        for dx in range(3):
            part = weight[2 - dy, (2 - dx) * chans:(3 - dx) * chans, :]
            flipped[dy, dx * chans:(dx + 1) * chans, :] = part.T
    acc[...] = jnp.zeros_like(acc)
    d_bias[...] = jnp.zeros_like(d_bias)

    def backward(n, carry):
        @pl.when(last)
        def _():
            gin[n] = cotangent[n]

        @pl.when(jnp.logical_not(last))
        def _():
            backward_copy(n).wait_recv()

        d_hidden = gin[n].astype(F32) * slope[n]
        d_conv = d_hidden * demod[n]
        spread(spread_g, d_conv)
        d_scaled = conv3(spread_g, flipped)
        gout[n] = (d_scaled * styles[n]).astype(BF16)

        @pl.when(jnp.logical_not(first))
        def _():
            backward_copy(n).start()

        d_style[n] = jnp.sum(d_scaled * fin[n].astype(F32), axis=0, keepdims=True)
        d_bias[...] += jnp.sum(d_hidden, axis=0, keepdims=True)
        d_demod[n] = jnp.sum(d_hidden * conv[n], axis=0, keepdims=True)
        turned = d_conv.astype(BF16).T
        for dy in range(3):
            acc[dy * chans:(dy + 1) * chans, :] += jnp.dot(
                turned, spread_x[n, dy * width:dy * width + pixels, :],
                preferred_element_type=F32,
            )
        return carry

    lax.fori_loop(0, count, backward, 0)

    wgrad_out[...] = acc[...].astype(BF16)
    style_rows = jnp.concatenate([styles[n] for n in range(count)], axis=0)
    demod_rows = jnp.concatenate([demod[n] for n in range(count)], axis=0)
    d_under = jnp.concatenate([d_demod[n] for n in range(count)], axis=0) * (
        -0.5 * demod_rows * demod_rows * demod_rows
    )
    d_rows = jnp.concatenate([d_style[n] for n in range(count)], axis=0)
    d_rows = d_rows + 2.0 * style_rows * exact(d_under, energy[...], NT)
    rows_out[0:count, :] = d_rows
    rows_out[count:2 * count, :] = d_under
    rows_out[2 * count:3 * count, :] = style_rows * style_rows
    rows_out[3 * count:3 * count + 1, :] = d_bias[...]
    latent_out[...] = exact(d_rows, affine[...], NT)

    def finish(n, carry):
        @pl.when(jnp.logical_not(last))
        def _():
            forward_copy(n).wait_send()

        @pl.when(jnp.logical_not(first))
        def _():
            backward_copy(n).wait_send()

        return carry

    lax.fori_loop(0, count, finish, 0)


def body(images, latent, weight, affine, biases, cotangent):
    count, height, width, chans = images.shape
    pixels = height * width
    kernel = weight[0]
    segments = lax.axis_size("segment")
    maps = (count, pixels, chans)
    row = (count, 1, chans)
    vmem = pl.BlockSpec(memory_space=pltpu.VMEM)
    dma = pltpu.SemaphoreType.DMA((count,))
    wgrad, rows, latent_part = pl.pallas_call(
        functools.partial(relay, segments, width),
        out_shape=(
            jax.ShapeDtypeStruct((3 * chans, 3 * chans), BF16),
            jax.ShapeDtypeStruct((3 * count + 1, chans), F32),
            jax.ShapeDtypeStruct(latent.shape, F32),
        ),
        in_specs=[vmem] * 6,
        out_specs=(vmem, vmem, vmem),
        scratch_shapes=[
            pltpu.VMEM(maps, BF16), pltpu.VMEM(maps, BF16),
            pltpu.VMEM(maps, BF16), pltpu.VMEM(maps, BF16),
            pltpu.VMEM((count, pixels + 2 * width, 3 * chans), BF16),
            pltpu.VMEM(maps, F32), pltpu.VMEM(maps, F32),
            pltpu.VMEM((3, 3 * chans, chans), BF16),
            pltpu.VMEM((pixels + 2 * width, 3 * chans), BF16),
            pltpu.VMEM((3 * chans, 3 * chans), F32),
            pltpu.VMEM((chans, chans), F32),
            pltpu.VMEM(row, F32), pltpu.VMEM(row, F32), pltpu.VMEM(row, F32),
            pltpu.VMEM(row, F32), pltpu.VMEM((1, chans), F32),
            dma, dma, dma, dma,
        ],
        compiler_params=pltpu.CompilerParams(
            collective_id=0, has_side_effects=True, vmem_limit_bytes=40 * 1024 * 1024
        ),
    )(
        images.reshape(maps), latent, kernel.reshape(3, 3 * chans, chans), affine[0], biases,
        cotangent.reshape(maps),
    )
    wgrad = lax.psum(wgrad, "dp").astype(F32)
    wgrad = wgrad.reshape(3, chans, 3, chans).transpose(0, 2, 3, 1)
    every = lax.all_gather(rows, "dp")
    latents = lax.all_gather(latent, "dp", tiled=True)
    d_rows = every[:, :count].reshape(-1, chans)
    d_under = every[:, count:2 * count].reshape(-1, chans)
    squares = every[:, 2 * count:3 * count].reshape(-1, chans)
    d_bias = jnp.sum(every[:, 3 * count], axis=0)
    wgrad = wgrad + 2.0 * kernel.astype(F32) * exact(squares, d_under, TN)
    d_affine = exact(latents, d_rows, TN)
    latent_total = lax.psum(latent_part, "segment")
    return (wgrad[None], d_affine[None], d_bias[None], latent_total)


def solution(mesh):
    placed = (
        P("dp", None, None, None),
        P("dp", None),
        P("segment", None, None, None, None),
        P("segment", None, None),
        P("segment", None),
        P("dp", None, None, None),
    )
    return jax.shard_map(
        body,
        mesh=mesh,
        in_specs=placed,
        out_specs=(
            P("segment", None, None, None, None),
            P("segment", None, None),
            P("segment", None),
            P("dp", None),
        ),
        check_vma=False,
    )
```

time: 329 us -> 141 us (0.43)
  matrix products: 85 us -> 1.05 us
  Pallas kernels: 0 us -> 55.7 us
  local copies, waits for them, and re-layouts: 65.3 us -> 13.5 us
  starting transfers between devices: 40.1 us -> 0.04 us
  waiting for transfers between devices: 60.3 us -> 24.8 us
  other arithmetic: 27.8 us -> 3.43 us
  blocking collectives: 31.3 us -> 27.5 us
    pallas_call x0 -> x1, Pallas kernels: none -> 55.7 us  [body(): pl.pallas_call(functools.partial(relay, segments, width), out_shape=(jax....]
    conv_general_dilated x28 -> x0, matrix products: 53 us -> none  [synth_layer(): lax.conv_general_dilated(scaled, kernel, (1, 1), 'SAME', dimension_number...]
    ppermute x14 -> x0, starting transfers between devices: 40.1 us -> none  [from_behind(): lax.ppermute(value, axis, [(source, source + steps) for source in range(l...]
    dot_general x42 -> x2, matrix products: 32 us -> 1.05 us  [exact(): lax.dot_general(a, b, dims, precision=lax.Precision.HIGHEST, preferred_el...]
    psum x2 -> x1, blocking collectives: 31.3 us -> 9.06 us  [body(): latent_total = lax.psum(latent_part, 'segment')]
    dynamic_slice x28 -> x0, local copies, waits for them, and re-layouts: 18.6 us -> none  [the longest x7 6.5 us: forward_tick(): first_input = lax.dynamic_slice_in_dim(images, clipped * MICRO, MICRO, 0)]
    psum x1, waiting for transfers between devices: 43.4 us -> 24.8 us  [body(): wgrad = lax.psum(wgrad, 'dp').astype(F32)]
    all_gather x0 -> x2, blocking collectives: none -> 18.5 us  [the longest x1 9.23 us: body(): every = lax.all_gather(rows, 'dp')]
  transfers between devices with their start and end apart: 15 -> 1, of which waited for: 8 -> 1; matrix products, arithmetic and copies ran while one was open for 24% -> 4% of each run, Pallas kernels for 0% -> 0%
where the time goes in v1:
time: 141 us; the launch traced here: 140 us
  Pallas kernels  55.7 us (40%)
  blocking collectives  27.5 us (20%)
  waiting for transfers between devices  24.8 us (18%)
  between operations  14.1 us (10%)
  local copies, waits for them, and re-layouts  13.5 us (10%)
  other arithmetic  3.43 us (2%)
    pallas_call x1, Pallas kernels, body(): pl.pallas_call(functools.partial(relay, segments, width), out_shape=(jax....  55.7 us
    psum x1, waiting for transfers between devices, body(): wgrad = lax.psum(wgrad, 'dp').astype(F32)  24.8 us
    unnamed x20, local copies, waits for them, and re-layouts  11.4 us
    all_gather x1, blocking collectives, body(): every = lax.all_gather(rows, 'dp')  9.23 us
    all_gather x1, blocking collectives, body(): latents = lax.all_gather(latent, 'dp', tiled=True)  9.22 us
    psum x1, blocking collectives, body(): latent_total = lax.psum(latent_part, 'segment')  9.06 us
    broadcast_in_dim x1, other arithmetic, body(): return (wgrad[None], d_affine[None], d_bias[None], latent_total)  2.84 us
  transfers between devices with their start and end apart: 1, of which 1 were waited for; matrix products, arithmetic and copies ran while one was open for 4% of the time, Pallas kernels for 0%

profile of v1, /device:TPU:0, one launch (start us, length us, event | category | flops | bytes accessed | tf_op | source)
XLA Modules:
  0.0 140.1 jit_solution(1943735309016991936)
XLA Ops:
  7.2 0.0 all-reduce.2.cloned.1.call-start
  7.2 0.0 copy-start
  7.2 1.3 copy-done
  8.5 0.0 copy-start.2
  8.5 1.0 copy-done.2
  9.5 0.0 copy-start.3
  9.5 1.0 copy-done.3
  10.6 0.0 copy-start.4
  10.6 1.0 copy-done.4
  11.6 0.0 copy-start.5
  11.6 0.7 copy-done.5
  12.3 0.0 copy-start.7
  12.3 0.7 copy-done.7
  13.0 55.7 %shard_map.93 = (bf16[768,768]{1,0:T(8,128)(2,1)S(1)}, f32[13,256]{1,0:T(8,128)S(1)}, f32[4,512]{1,0:T(4,128)S(1)}) custom-call(bf16[4,256,256]{2,1,0:T(8,128)(2,1)S(1)} %bitcast.24, f32[4,512]{1,0:T(4,128)S(1)} %copy-done.5, bf16[3,768,256]{2,1,0:T(8,128)(2,1)S(1)} %bitcast.23, f32[512,256]{1,0:T(8,128)S(1)} %bitcast.25, f32[1,256]{1,0:T(1,128)S(1)} %copy-done.7, ...), custom_call_target="tpu_custom_call" | custom-call | tf_op jit(solution)/shard_map/pallas_call | solution.py:199
  68.7 0.0 copy-start.1
  68.7 1.9 %reshape.28 = bf16[3,256,3,256]{3,2,1,0:T(4,128)(2,1)} reshape(bf16[768,768]{1,0:T(8,128)(2,1)S(1)} %get-tuple-element.7) | data formatting | bytes 2359296 | tf_op jit(solution)/shard_map/reshape | solution.py:229
  70.6 0.0 all-reduce.2.cloned.1.call-update
  70.6 0.0 copy-done.1
  70.6 0.0 copy-start.6
  70.6 2.2 %copy.20 = bf16[1,3,3,256,256]{3,2,4,1,0:T(4,128)(2,1)} copy(bf16[1,3,3,256,256]{4,3,2,1,0:T(8,128)(2,1)S(1)} %copy-done.1) | data formatting | bytes 2359296 | tf_op args[2]
  72.8 9.2 %all-gather.1 = f32[8,13,256]{2,1,0:T(8,128)S(1)} all-gather(f32[1,13,256]{2,1,0:T(8,128)S(1)} %bitcast.28), channel_id=2, replica_groups=mesh['segment'=4,'dp'=8] {'dp'}, dimensions={0}, use_global_device_ids=true | all-gather | bytes 119808 | tf_op jit(solution)/shard_map/all_gather | solution.py:230
  82.0 0.4 fusion.2
  82.5 0.1 copy.21
  82.6 0.0 copy-done.6
  82.6 9.2 %all-gather.2 = f32[8,4,512]{2,1,0:T(4,128)S(1)} all-gather(f32[1,4,512]{2,1,0:T(4,128)S(1)} %bitcast.27), channel_id=1, replica_groups=mesh['segment'=4,'dp'=8] {'dp'}, dimensions={0}, use_global_device_ids=true | all-gather | bytes 73728 | tf_op jit(solution)/shard_map/all_gather | solution.py:231
  91.9 0.6 convolution_bitcast_fusion
  92.5 1.0 copy.23
  93.5 9.1 %psum.15 = f32[4,512]{1,0:T(4,128)} all-reduce(f32[4,512]{1,0:T(4,128)S(1)} %get-tuple-element.9), channel_id=1, replica_groups=mesh['segment'=4,'dp'=8] {'segment'}, use_global_device_ids=true, to_apply=%region_2.0 | all-reduce | flops 2048 | bytes 16384 | tf_op jit(solution)/shard_map/psum | solution.py:238
  102.6 0.6 slice_reduce_fusion
  103.2 24.8 %all-reduce.2.cloned.1.call-done = bf16[3,3,256,256]{2,1,3,0:T(4,128)(2,1)} async-done(((bf16[3,3,256,256]{2,1,3,0:T(4,128)(2,1)}), bf16[3,3,256,256]{2,1,3,0:T(4,128)(2,1)}) %all-reduce.2.cloned.1.call-update) | async-done | bytes 1179664 | tf_op jit(solution)/shard_map/psum | solution.py:228
  127.9 2.8 %fusion.1 = f32[1,3,3,256,256]{3,2,4,1,0:T(4,128)S(1)} fusion(bf16[3,3,256,256]{2,1,3,0:T(4,128)(2,1)} %all-reduce.2.cloned.1.call-done, bf16[1,3,3,256,256]{3,2,4,1,0:T(4,128)(2,1)} %copy.20, f32[256,256]{0,1:T(8,128)S(1)} %copy.21), kind=kLoop, calls=%fused_computation.2 | loop fusion | flops 2359296 | bytes 4980736 | tf_op jit(solution)/shard_map/broadcast_in_dim | solution.py:239
  130.8 2.5 %copy.22 = f32[1,3,3,256,256]{4,3,2,1,0:T(8,128)} copy(f32[1,3,3,256,256]{3,2,4,1,0:T(4,128)S(1)} %fusion.1) | data formatting | bytes 4718592
  (3 shorter events, 0.0 us)
Async XLA Ops:
  7.2 120.8 %all-reduce.2.cloned.1.call-start = ((), (), s32[]{:S(2)}) async-start(), calls=%async_computation | async-start | bytes 3145728 | tf_op jit(solution)/shard_map/psum | solution.py:228
  7.2 1.3 copy-start
  8.5 1.0 copy-start.2
  9.5 1.0 copy-start.3
  10.6 1.0 copy-start.4
  11.6 0.7 copy-start.5
  12.3 0.7 copy-start.7
  68.7 1.9 %copy-start.1 = (bf16[1,3,3,256,256]{4,3,2,1,0:T(8,128)(2,1)S(1)}, bf16[1,3,3,256,256]{4,3,2,1,0:T(8,128)(2,1)}, u32[]{:S(2)}) copy-start(bf16[1,3,3,256,256]{4,3,2,1,0:T(8,128)(2,1)} %param.8) | copy-start | bytes 3538948
  70.6 12.0 %copy-start.6 = (f32[4,512]{1,0:T(4,128)S(1)}, f32[4,512]{1,0:T(4,128)}, u32[]{:S(2)}) copy-start(f32[4,512]{1,0:T(4,128)} %latent.1) | copy-start | bytes 24580
Sparse Core Ops, SparseCore 0:
  70.7 57.1 all-reduce.1

commit v2 on v1

v2 whole, which is shorter than its diff:
```python
import functools
import math

import jax
import jax.numpy as jnp
from jax import lax
from jax.experimental import pallas as pl
from jax.experimental.pallas import tpu as pltpu
from jax.sharding import PartitionSpec as P

GAIN = math.sqrt(2.0)
MESH = pl.DeviceIdType.MESH
F32 = jnp.float32
BF16 = jnp.bfloat16
NN = (((1,), (0,)), ((), ()))
NT = (((1,), (1,)), ((), ()))
TN = (((0,), (0,)), ((), ()))


def exact(a, b, dims):
    return lax.dot_general(
        a, b, dims, precision=lax.Precision.HIGHEST, preferred_element_type=F32
    )


def relay(
    segments, replicas, width,
    images, latent, weight_in, affine_in, biases_in, cotangent,
    wgrad, energy_grad, affine_grad, bias_grad, latent_grad,
    fin, fout, gin, gout, weight, affine, biases, latents,
    spread_x, turned_x, conv, slope, flipped, spread_g, acc, energy,
    styles, demod, d_demod, d_style, d_bias, rows, parts,
    pair_out, pair_in, chip_out, chip_in, own,
    f_send, f_recv, g_send, g_recv, loads, l_send, l_recv, r_send, r_recv, p_send, p_recv,
    a_send, a_recv, b_send, b_recv, c_send, c_recv, d_send, d_recv,
):
    count, pixels, chans = fin.shape
    chips = replicas // 2
    share = acc.shape[0] // replicas
    seg, me = lax.axis_index("segment"), lax.axis_index("dp")
    chip, core = me // 2, lax.rem(me, 2)
    partner = me + 1 - 2 * core
    first, last = seg == 0, seg == segments - 1
    up, down = jnp.minimum(seg + 1, segments - 1), jnp.maximum(seg - 1, 0)

    def remote(src, dst, send, recv, **device):
        return pltpu.make_async_remote_copy(
            src_ref=src, dst_ref=dst, send_sem=send, recv_sem=recv,
            device_id=device, device_id_type=MESH,
        )

    load_weight = pltpu.make_async_copy(weight_in, weight, loads.at[0])
    load_affine = pltpu.make_async_copy(affine_in, affine, loads.at[1])
    load_latent = pltpu.make_async_copy(latent, latents.at[me], loads.at[2])
    load_biases = pltpu.make_async_copy(biases_in, biases, loads.at[3])
    load_images = pltpu.make_async_copy(images, fin, loads.at[4])
    load_cotangent = pltpu.make_async_copy(cotangent, gin, loads.at[5])
    load_weight.start()
    load_affine.start()
    load_latent.start()
    load_biases.start()

    @pl.when(first)
    def _():
        load_images.start()

    @pl.when(last)
    def _():
        load_cotangent.start()

    barrier = pltpu.get_barrier_semaphore()
    for k in range(1, replicas):
        pl.semaphore_signal(
            barrier, inc=1, device_id={"dp": lax.rem(me + k, replicas)}, device_id_type=MESH
        )
    for k in range(1, segments):
        pl.semaphore_signal(
            barrier, inc=1, device_id={"segment": lax.rem(seg + k, segments)}, device_id_type=MESH
        )

    def forward_copy(n):
        return remote(fout.at[n], fin.at[n], f_send.at[n], f_recv.at[n], segment=up)

    def backward_copy(n):
        return remote(gout.at[n], gin.at[n], g_send.at[n], g_recv.at[n], segment=down)

    def latent_copy(k, owner):
        return remote(
            latents.at[owner], latents.at[owner], l_send.at[k], l_recv.at[k],
            dp=lax.rem(me + k, replicas),
        )

    def rows_copy(k, owner):
        return remote(
            rows.at[owner], rows.at[owner], r_send.at[k], r_recv.at[k],
            dp=lax.rem(me + k, replicas),
        )

    def parts_copy(k, owner):
        return remote(
            parts.at[owner], parts.at[owner], p_send.at[k], p_recv.at[k],
            segment=lax.rem(seg + k, segments),
        )

    column = lax.rem(lax.broadcasted_iota(jnp.int32, (pixels, chans), 0), width)
    at_left, at_right = column == 0, column == width - 1
    middle = slice(width, width + pixels)

    def spread(target, value):
        target[middle, chans:2 * chans] = value.astype(BF16)
        target[middle, :chans] = jnp.where(at_left, 0.0, pltpu.roll(value, 1, 0)).astype(BF16)
        target[middle, 2 * chans:] = jnp.where(
            at_right, 0.0, pltpu.roll(value, pixels - 1, 0)
        ).astype(BF16)

    def conv3(source, kernel):
        total = jnp.dot(source[0:pixels, :], kernel[0], preferred_element_type=F32)
        for dy in (1, 2):
            total += jnp.dot(
                source[dy * width:dy * width + pixels, :], kernel[dy], preferred_element_type=F32
            )
        return total

    edge = jnp.zeros((width, 3 * chans), BF16)
    for n in range(count):
        for target in (spread_x, spread_g):
            target[n, 0:width, :] = edge
            target[n, width + pixels:, :] = edge
    d_bias[...] = jnp.zeros_like(d_bias)
    load_weight.wait()
    total = jnp.zeros((chans, chans), F32)
    for dy in range(3):
        for dx in range(3):
            total += jnp.square(weight[dy, dx * chans:(dx + 1) * chans, :].astype(F32))
    energy[...] = total
    load_affine.wait()
    load_latent.wait()
    load_biases.wait()
    style_rows = exact(latents[me], affine[...], NN) + 1.0
    demod_rows = lax.rsqrt(exact(style_rows * style_rows, total, NN) + 1e-08)
    for n in range(count):
        styles[n] = style_rows[n:n + 1, :]
        demod[n] = demod_rows[n:n + 1, :]

    def flip():
        for dy in range(3):
            for dx in range(3):
                part = weight[2 - dy, (2 - dx) * chans:(3 - dx) * chans, :]
                flipped[dy, dx * chans:(dx + 1) * chans, :] = part.T

    @pl.when(first)
    def _():
        load_images.wait()

    @pl.when(last)
    def _():
        flip()
        load_cotangent.wait()

    pl.semaphore_wait(barrier, replicas + segments - 2)

    def forward(n):
        @pl.when(jnp.logical_not(first))
        def _():
            forward_copy(n).wait_recv()

        spread(spread_x.at[n], fin[n].astype(F32) * styles[n])
        convolved = conv3(spread_x.at[n], weight)
        conv[n] = convolved
        hidden = convolved * demod[n] + biases[...]
        gate = jnp.tanh(hidden)
        fout[n] = (GAIN * hidden * (0.6 + 0.4 * gate)).astype(BF16)

        @pl.when(jnp.logical_not(last))
        def _():
            forward_copy(n).start()

        slope[n] = GAIN * (0.6 + 0.4 * gate + 0.4 * hidden * (1.0 - gate * gate))

    def backward(n):
        d_hidden = gin[n].astype(F32) * slope[n]
        spread(spread_g.at[n], d_hidden * demod[n])
        d_scaled = conv3(spread_g.at[n], flipped)
        gout[n] = (d_scaled * styles[n]).astype(BF16)

        @pl.when(jnp.logical_not(first))
        def _():
            backward_copy(n).start()

        d_style[n] = jnp.sum(d_scaled * fin[n].astype(F32), axis=0, keepdims=True)
        d_bias[...] += jnp.sum(d_hidden, axis=0, keepdims=True)
        d_demod[n] = jnp.sum(d_hidden * conv[n], axis=0, keepdims=True)

    def forward_step(n, carry):
        forward(n)

        @pl.when(last)
        def _():
            backward(n)

        turned_x[n] = spread_x[n, middle, chans:2 * chans].T
        return carry

    lax.fori_loop(0, count, forward_step, 0)

    @pl.when(jnp.logical_not(last))
    def _():
        flip()

    for k in range(1, replicas):
        latent_copy(k, me).start()
    acc[...] = jnp.zeros_like(acc)

    def backward_step(n, carry):
        @pl.when(jnp.logical_not(last))
        def _():
            backward_copy(n).wait_recv()
            backward(n)

        for dy in range(3):
            block = jnp.dot(
                turned_x[n], spread_g[n, dy * width:dy * width + pixels, :],
                preferred_element_type=F32,
            )
            for dx in range(3):
                start = ((2 - dy) * 3 + 2 - dx) * chans
                acc[start:start + chans, :] += block[:, dx * chans:(dx + 1) * chans]
        return carry

    lax.fori_loop(0, count, backward_step, 0)

    def acc_share(half, q):
        start = pl.multiple_of((half * chips + q) * share, share)
        return acc[pl.ds(start, share), :]

    def pair_copy(k):
        return remote(pair_out.at[k], pair_in.at[k], a_send.at[k], a_recv.at[k], dp=partner)

    def chip_copy(k):
        return remote(
            chip_out.at[k], chip_in.at[k], b_send.at[k], b_recv.at[k],
            dp=2 * lax.rem(chip + k, chips) + core,
        )

    def shard_copy(k, q):
        return remote(
            wgrad.at[core, q], wgrad.at[core, q], c_send.at[k], c_recv.at[k],
            dp=2 * lax.rem(chip + k, chips) + core,
        )

    def relay_copy(k, half, q):
        return remote(
            wgrad.at[half, q], wgrad.at[half, q], d_send.at[k], d_recv.at[k], dp=partner
        )

    order = list(range(1, chips)) + [0]
    for k in order:
        pair_out[k] = acc_share(1 - core, lax.rem(chip + k, chips)).astype(BF16)
        pair_copy(k).start()
    for k in order:
        pair_copy(k).wait_recv()
        both = acc_share(core, lax.rem(chip + k, chips)) + pair_in[k].astype(F32)
        if k:
            chip_out[k] = both.astype(BF16)
            chip_copy(k).start()
        else:
            own[...] = both

    style_rows = jnp.concatenate([styles[n] for n in range(count)], axis=0)
    demod_rows = jnp.concatenate([demod[n] for n in range(count)], axis=0)
    d_under = jnp.concatenate([d_demod[n] for n in range(count)], axis=0) * (
        -0.5 * demod_rows * demod_rows * demod_rows
    )
    d_rows = jnp.concatenate([d_style[n] for n in range(count)], axis=0)
    d_rows = d_rows + 2.0 * style_rows * exact(d_under, energy[...], NT)
    rows[me, 0] = d_rows
    rows[me, 1] = d_under
    rows[me, 2] = style_rows * style_rows
    rows[me, 3] = jnp.broadcast_to(d_bias[...], (count, chans))
    for k in range(1, replicas):
        rows_copy(k, me).start()
    parts[seg] = exact(d_rows, affine[...], NT)
    for k in range(1, segments):
        parts_copy(k, seg).start()

    reduced = own[...]
    for k in range(1, chips):
        chip_copy(k).wait_recv()
        reduced += chip_in[k].astype(F32)
    wgrad[core, chip] = reduced.astype(BF16)
    for k in range(1, chips):
        shard_copy(k, chip).start()
    relay_copy(0, core, chip).start()

    for k in range(1, replicas):
        owner = lax.rem(me + replicas - k, replicas)
        latent_copy(k, owner).wait_recv()
        rows_copy(k, owner).wait_recv()
    d_rows = jnp.concatenate([rows[d, 0] for d in range(replicas)], axis=0)
    d_under = jnp.concatenate([rows[d, 1] for d in range(replicas)], axis=0)
    squares = jnp.concatenate([rows[d, 2] for d in range(replicas)], axis=0)
    every = jnp.concatenate([latents[d] for d in range(replicas)], axis=0)
    energy_grad[...] = 2.0 * exact(squares, d_under, TN)
    affine_grad[...] = exact(every, d_rows, TN)
    bias_total = rows[0, 3]
    for d in range(1, replicas):
        bias_total += rows[d, 3]
    bias_grad[...] = bias_total[0:1, :]

    for k in range(1, chips):
        q = lax.rem(chip + chips - k, chips)
        shard_copy(k, q).wait_recv()
        relay_copy(k, core, q).start()

    for k in range(1, segments):
        parts_copy(k, lax.rem(seg + segments - k, segments)).wait_recv()
    latent_total = parts[0]
    for s in range(1, segments):
        latent_total += parts[s]
    latent_grad[...] = latent_total

    for k in range(chips):
        relay_copy(k, 1 - core, lax.rem(chip + chips - k, chips)).wait_recv()

    def finish(n, carry):
        @pl.when(jnp.logical_not(last))
        def _():
            forward_copy(n).wait_send()

        @pl.when(jnp.logical_not(first))
        def _():
            backward_copy(n).wait_send()

        return carry

    lax.fori_loop(0, count, finish, 0)
    for k in range(1, replicas):
        latent_copy(k, me).wait_send()
        rows_copy(k, me).wait_send()
    for k in range(1, segments):
        parts_copy(k, seg).wait_send()
    for k in range(chips):
        pair_copy(k).wait_send()
        relay_copy(k, core, lax.rem(chip + chips - k, chips)).wait_send()
        if k:
            chip_copy(k).wait_send()
            shard_copy(k, chip).wait_send()


def body(images, latent, weight, affine, biases, cotangent):
    count, height, width, chans = images.shape
    pixels = height * width
    kernel = weight[0]
    segments, replicas = lax.axis_size("segment"), lax.axis_size("dp")
    chips = replicas // 2
    taps = 9 * chans
    share = taps // replicas
    maps = (count, pixels, chans)
    row = (count, 1, chans)
    tall = (count, pixels + 2 * width, 3 * chans)
    vmem = pl.BlockSpec(memory_space=pltpu.VMEM)
    here = pl.BlockSpec(memory_space=pl.ANY)
    dma = pltpu.SemaphoreType.DMA
    wgrad, energy_grad, affine_grad, bias_grad, latent_grad = pl.pallas_call(
        functools.partial(relay, segments, replicas, width),
        out_shape=(
            jax.ShapeDtypeStruct((2, chips, share, chans), BF16),
            jax.ShapeDtypeStruct((chans, chans), F32),
            jax.ShapeDtypeStruct(affine.shape[1:], F32),
            jax.ShapeDtypeStruct((1, chans), F32),
            jax.ShapeDtypeStruct(latent.shape, F32),
        ),
        in_specs=[here] * 6,
        out_specs=(vmem,) * 5,
        scratch_shapes=[
            pltpu.VMEM(maps, BF16), pltpu.VMEM(maps, BF16),
            pltpu.VMEM(maps, BF16), pltpu.VMEM(maps, BF16),
            pltpu.VMEM((3, 3 * chans, chans), BF16),
            pltpu.VMEM(affine.shape[1:], F32),
            pltpu.VMEM((1, chans), F32),
            pltpu.VMEM((replicas,) + latent.shape, F32),
            pltpu.VMEM(tall, BF16),
            pltpu.VMEM((count, chans, pixels), BF16),
            pltpu.VMEM(maps, F32), pltpu.VMEM(maps, F32),
            pltpu.VMEM((3, 3 * chans, chans), BF16),
            pltpu.VMEM(tall, BF16),
            pltpu.VMEM((taps, chans), F32),
            pltpu.VMEM((chans, chans), F32),
            pltpu.VMEM(row, F32), pltpu.VMEM(row, F32), pltpu.VMEM(row, F32),
            pltpu.VMEM(row, F32), pltpu.VMEM((1, chans), F32),
            pltpu.VMEM((replicas, 4, count, chans), F32),
            pltpu.VMEM((segments,) + latent.shape, F32),
            pltpu.VMEM((chips, share, chans), BF16), pltpu.VMEM((chips, share, chans), BF16),
            pltpu.VMEM((chips, share, chans), BF16), pltpu.VMEM((chips, share, chans), BF16),
            pltpu.VMEM((share, chans), F32),
            dma((count,)), dma((count,)), dma((count,)), dma((count,)), dma((6,)),
            dma((replicas,)), dma((replicas,)), dma((replicas,)), dma((replicas,)),
            dma((segments,)), dma((segments,)),
            dma((chips,)), dma((chips,)), dma((chips,)), dma((chips,)),
            dma((chips,)), dma((chips,)), dma((chips,)), dma((chips,)),
        ],
        compiler_params=pltpu.CompilerParams(
            collective_id=0, has_side_effects=True, vmem_limit_bytes=56 * 1024 * 1024
        ),
    )(
        images.reshape(maps), latent, kernel.reshape(3, 3 * chans, chans), affine[0], biases,
        cotangent.reshape(maps),
    )
    wgrad = wgrad.reshape(kernel.shape).astype(F32) + kernel.astype(F32) * energy_grad
    return (wgrad[None], affine_grad[None], bias_grad, latent_grad)


def solution(mesh):
    placed = (
        P("dp", None, None, None),
        P("dp", None),
        P("segment", None, None, None, None),
        P("segment", None, None),
        P("segment", None),
        P("dp", None, None, None),
    )
    return jax.shard_map(
        body,
        mesh=mesh,
        in_specs=placed,
        out_specs=(
            P("segment", None, None, None, None),
            P("segment", None, None),
            P("segment", None),
            P("dp", None),
        ),
        check_vma=False,
    )
```

time: 141 us -> 72.6 us (0.51)
  blocking collectives: 27.5 us -> 0 us
  waiting for transfers between devices: 24.8 us -> 0 us
  between operations: 14.1 us -> 0.68 us
  local copies, waits for them, and re-layouts: 13.5 us -> 1.97 us
  Pallas kernels: 55.7 us -> 66.7 us
    psum x1 -> x0, waiting for transfers between devices: 24.8 us -> none  [body(): wgrad = lax.psum(wgrad, 'dp').astype(F32)]
    all_gather x2 -> x0, blocking collectives: 18.5 us -> none  [the longest x1 9.23 us: body(): every = lax.all_gather(rows, 'dp')]
    pallas_call x1, Pallas kernels: 55.7 us -> 66.7 us  [body(): pl.pallas_call(functools.partial(relay, segments, replicas, width), out_s...]
    unnamed x20 -> x11, local copies, waits for them, and re-layouts: 11.4 us -> 1.97 us
    psum x1 -> x0, blocking collectives: 9.06 us -> none  [body(): latent_total = lax.psum(latent_part, 'segment')]
    add x0 -> x1, other arithmetic: none -> 3.11 us  [body(): wgrad.reshape(kernel.shape).astype(F32) + kernel.astype(F32) * energy_grad]
    broadcast_in_dim x1 -> x0, other arithmetic: 2.84 us -> none  [body(): return (wgrad[None], d_affine[None], d_bias[None], latent_total)]
    reshape x2 -> x0, local copies, waits for them, and re-layouts: 1.9 us -> none  [the longest x1 1.89 us: body(): wgrad = wgrad.reshape(3, chans, 3, chans).transpose(0, 2, 3, 1)]
  transfers between devices with their start and end apart: 1 -> 0, of which waited for: 1 -> 0; matrix products, arithmetic and copies ran while one was open for 4% -> 0% of each run, Pallas kernels for 0% -> 0%
where the time goes in v2:
time: 72.6 us; the launch traced here: 72.5 us
  Pallas kernels  66.7 us (92%)
  other arithmetic  3.11 us (4%)
  local copies, waits for them, and re-layouts  1.97 us (3%)
    pallas_call x1, Pallas kernels, body(): pl.pallas_call(functools.partial(relay, segments, replicas, width), out_s...  66.7 us
    add x1, other arithmetic, body(): wgrad.reshape(kernel.shape).astype(F32) + kernel.astype(F32) * energy_grad  3.11 us
    unnamed x11, local copies, waits for them, and re-layouts  1.97 us

profile of v2, /device:TPU:0, one launch (start us, length us, event | category | flops | bytes accessed | tf_op | source)
XLA Modules:
  0.0 72.5 jit_solution(17869546893891456856)
XLA Ops:
  0.6 0.0 copy-start
  0.6 66.7 %shard_map.93 = (bf16[2,4,288,256]{3,2,1,0:T(8,128)(2,1)}, f32[256,256]{1,0:T(8,128)}, f32[512,256]{1,0:T(8,128)}, f32[1,256]{1,0:T(1,128)}, f32[4,512]{1,0:T(4,128)}) custom-call(bf16[4,256,256]{2,1,0:T(8,128)(2,1)} %bitcast.9, f32[4,512]{1,0:T(4,128)} %latent.1, bf16[3,768,256]{2,1,0:T(8,128)(2,1)} %bitcast.7, f32[512,256]{1,0:T(8,128)} %bitcast.10, ...), custom_call_target="tpu_custom_call" | custom-call | tf_op jit(solution)/shard_map/pallas_call | solution.py:364
  67.4 0.0 copy-done
  67.4 0.0 copy-start.1
  67.4 0.0 copy-start.3
  67.4 0.0 copy-start.2
  67.4 3.1 %convert_add_fusion = f32[1,3,3,256,256]{4,3,2,1,0:T(8,128)} fusion(bf16[1,3,3,256,256]{4,3,2,1,0:T(8,128)(2,1)} %bitcast.8, bf16[1,3,3,256,256]{4,3,2,1,0:T(8,128)(2,1)S(1)} %copy-done, f32[256,256]{1,0:T(8,128)} %get-tuple-element.10), kind=kLoop, calls=%fused_computation | loop fusion | flops 2359296 | bytes 4980736 | tf_op jit(solution)/shard_map/add | solution.py:409
  70.5 0.0 copy-done.1
  70.5 0.8 %copy.13 = f32[1,512,256]{2,1,0:T(8,128)} copy(f32[1,512,256]{2,1,0:T(8,128)S(1)} %bitcast.12) | data formatting | bytes 1048576
  71.3 0.0 copy-done.3
  71.3 0.6 copy.14
  71.9 0.0 copy-done.2
  71.9 0.6 copy.15
Async XLA Ops:
  0.6 66.8 %copy-start = (bf16[1,3,3,256,256]{4,3,2,1,0:T(8,128)(2,1)S(1)}, bf16[1,3,3,256,256]{4,3,2,1,0:T(8,128)(2,1)}, u32[]{:S(2)}) copy-start(bf16[1,3,3,256,256]{4,3,2,1,0:T(8,128)(2,1)} %param.8) | copy-start | bytes 3538948
  67.4 3.1 %copy-start.1 = (f32[512,256]{1,0:T(8,128)S(1)}, f32[512,256]{1,0:T(8,128)}, u32[]{:S(2)}) copy-start(f32[512,256]{1,0:T(8,128)} %get-tuple-element.11) | copy-start | bytes 1572868
  67.4 3.9 %copy-start.3 = (f32[1,256]{1,0:T(1,128)S(1)}, f32[1,256]{1,0:T(1,128)}, u32[]{:S(2)}) copy-start(f32[1,256]{1,0:T(1,128)} %get-tuple-element.20) | copy-start | bytes 3076
  67.4 4.5 %copy-start.2 = (f32[4,512]{1,0:T(4,128)S(1)}, f32[4,512]{1,0:T(4,128)}, u32[]{:S(2)}) copy-start(f32[4,512]{1,0:T(4,128)} %get-tuple-element.21) | copy-start | bytes 24580

commit v3 on v2

--- a/solution.py
+++ b/solution.py
@@ -41,7 +41,6 @@
     chip, core = me // 2, lax.rem(me, 2)
     partner = me + 1 - 2 * core
     first, last = seg == 0, seg == segments - 1
-    up, down = jnp.minimum(seg + 1, segments - 1), jnp.maximum(seg - 1, 0)
 
     def remote(src, dst, send, recv, **device):
         return pltpu.make_async_remote_copy(
@@ -78,11 +77,25 @@
             barrier, inc=1, device_id={"segment": lax.rem(seg + k, segments)}, device_id_type=MESH
         )
 
-    def forward_copy(n):
-        return remote(fout.at[n], fin.at[n], f_send.at[n], f_recv.at[n], segment=up)
-
-    def backward_copy(n):
-        return remote(gout.at[n], gin.at[n], g_send.at[n], g_recv.at[n], segment=down)
+    def rows_of(cut, piece):
+        return (0, cut * width) if piece == 0 else (cut * width, pixels - cut * width)
+
+    def cut_at(hops):
+        return pixels // width // 2 + segments // 2 - 1 - hops
+
+    def forward_copy(n, piece, cut, to):
+        block = pl.ds(*rows_of(cut, piece))
+        return remote(
+            fout.at[n, block], fin.at[n, block], f_send.at[n, piece], f_recv.at[n, piece],
+            segment=to,
+        )
+
+    def backward_copy(n, piece, cut, to):
+        block = pl.ds(*rows_of(cut, piece))
+        return remote(
+            gout.at[n, block], gin.at[n, block], g_send.at[n, piece], g_recv.at[n, piece],
+            segment=to,
+        )
 
     def latent_copy(k, owner):
         return remote(
@@ -102,23 +115,25 @@
             segment=lax.rem(seg + k, segments),
         )
 
-    column = lax.rem(lax.broadcasted_iota(jnp.int32, (pixels, chans), 0), width)
-    at_left, at_right = column == 0, column == width - 1
     middle = slice(width, width + pixels)
 
-    def spread(target, value):
-        target[middle, chans:2 * chans] = value.astype(BF16)
-        target[middle, :chans] = jnp.where(at_left, 0.0, pltpu.roll(value, 1, 0)).astype(BF16)
-        target[middle, 2 * chans:] = jnp.where(
-            at_right, 0.0, pltpu.roll(value, pixels - 1, 0)
+    def spread(target, value, start):
+        size = value.shape[0]
+        column = lax.rem(lax.broadcasted_iota(jnp.int32, (size, chans), 0), width)
+        block = slice(width + start, width + start + size)
+        target[block, chans:2 * chans] = value.astype(BF16)
+        target[block, :chans] = jnp.where(
+            column == 0, 0.0, pltpu.roll(value, 1, 0)
         ).astype(BF16)
-
-    def conv3(source, kernel):
-        total = jnp.dot(source[0:pixels, :], kernel[0], preferred_element_type=F32)
+        target[block, 2 * chans:] = jnp.where(
+            column == width - 1, 0.0, pltpu.roll(value, size - 1, 0)
+        ).astype(BF16)
+
+    def conv3(source, kernel, start, size):
+        total = jnp.dot(source[start:start + size, :], kernel[0], preferred_element_type=F32)
         for dy in (1, 2):
-            total += jnp.dot(
-                source[dy * width:dy * width + pixels, :], kernel[dy], preferred_element_type=F32
-            )
+            at = start + dy * width
+            total += jnp.dot(source[at:at + size, :], kernel[dy], preferred_element_type=F32)
         return total
 
     edge = jnp.zeros((width, 3 * chans), BF16)
@@ -148,75 +163,50 @@
                 part = weight[2 - dy, (2 - dx) * chans:(3 - dx) * chans, :]
                 flipped[dy, dx * chans:(dx + 1) * chans, :] = part.T
 
-    @pl.when(first)
-    def _():
-        load_images.wait()
-
-    @pl.when(last)
-    def _():
-        flip()
-        load_cotangent.wait()
-
     pl.semaphore_wait(barrier, replicas + segments - 2)
 
-    def forward(n):
-        @pl.when(jnp.logical_not(first))
-        def _():
-            forward_copy(n).wait_recv()
-
-        spread(spread_x.at[n], fin[n].astype(F32) * styles[n])
-        convolved = conv3(spread_x.at[n], weight)
-        conv[n] = convolved
-        hidden = convolved * demod[n] + biases[...]
-        gate = jnp.tanh(hidden)
-        fout[n] = (GAIN * hidden * (0.6 + 0.4 * gate)).astype(BF16)
-
-        @pl.when(jnp.logical_not(last))
-        def _():
-            forward_copy(n).start()
-
-        slope[n] = GAIN * (0.6 + 0.4 * gate + 0.4 * hidden * (1.0 - gate * gate))
-
-    def backward(n):
-        d_hidden = gin[n].astype(F32) * slope[n]
-        spread(spread_g.at[n], d_hidden * demod[n])
-        d_scaled = conv3(spread_g.at[n], flipped)
-        gout[n] = (d_scaled * styles[n]).astype(BF16)
-
-        @pl.when(jnp.logical_not(first))
-        def _():
-            backward_copy(n).start()
-
-        d_style[n] = jnp.sum(d_scaled * fin[n].astype(F32), axis=0, keepdims=True)
-        d_bias[...] += jnp.sum(d_hidden, axis=0, keepdims=True)
-        d_demod[n] = jnp.sum(d_hidden * conv[n], axis=0, keepdims=True)
-
-    def forward_step(n, carry):
-        forward(n)
-
-        @pl.when(last)
-        def _():
-            backward(n)
-
-        turned_x[n] = spread_x[n, middle, chans:2 * chans].T
-        return carry
-
-    lax.fori_loop(0, count, forward_step, 0)
-
-    @pl.when(jnp.logical_not(last))
-    def _():
-        flip()
-
-    for k in range(1, replicas):
-        latent_copy(k, me).start()
-    acc[...] = jnp.zeros_like(acc)
-
-    def backward_step(n, carry):
-        @pl.when(jnp.logical_not(last))
-        def _():
-            backward_copy(n).wait_recv()
-            backward(n)
-
+    def forward(n, index):
+        cut = cut_at(index)
+        for piece in range(2):
+            start, size = rows_of(cut + 1, piece)
+            if index > 0:
+                forward_copy(n, piece, cut + 1, index - 1).wait_recv()
+            spread(
+                spread_x.at[n], fin[n, start:start + size, :].astype(F32) * styles[n], start
+            )
+            start, size = rows_of(cut, piece)
+            block = slice(start, start + size)
+            convolved = conv3(spread_x.at[n], weight, start, size)
+            hidden = convolved * demod[n] + biases[...]
+            gate = jnp.tanh(hidden)
+            if index < segments - 1:
+                fout[n, block, :] = (GAIN * hidden * (0.6 + 0.4 * gate)).astype(BF16)
+                forward_copy(n, piece, cut, index + 1).start()
+            conv[n, block, :] = convolved
+            slope[n, block, :] = GAIN * (0.6 + 0.4 * gate + 0.4 * hidden * (1.0 - gate * gate))
+
+    def backward(n, index):
+        cut = cut_at(segments - 1 - index)
+        for piece in range(2):
+            start, size = rows_of(cut + 1, piece)
+            block = slice(start, start + size)
+            if index < segments - 1:
+                backward_copy(n, piece, cut + 1, index + 1).wait_recv()
+            d_hidden = gin[n, block, :].astype(F32) * slope[n, block, :]
+            spread(spread_g.at[n], d_hidden * demod[n], start)
+            start, size = rows_of(cut, piece)
+            out = slice(start, start + size)
+            d_scaled = conv3(spread_g.at[n], flipped, start, size)
+            if index > 0:
+                gout[n, out, :] = (d_scaled * styles[n]).astype(BF16)
+                backward_copy(n, piece, cut, index - 1).start()
+            style_part = jnp.sum(d_scaled * fin[n, out, :].astype(F32), axis=0, keepdims=True)
+            demod_part = jnp.sum(d_hidden * conv[n, block, :], axis=0, keepdims=True)
+            d_style[n] = style_part if piece == 0 else d_style[n] + style_part
+            d_demod[n] = demod_part if piece == 0 else d_demod[n] + demod_part
+            d_bias[...] += jnp.sum(d_hidden, axis=0, keepdims=True)
+
+    def add_weight_grad(n):
         for dy in range(3):
             block = jnp.dot(
                 turned_x[n], spread_g[n, dy * width:dy * width + pixels, :],
@@ -225,9 +215,50 @@
             for dx in range(3):
                 start = ((2 - dy) * 3 + 2 - dx) * chans
                 acc[start:start + chans, :] += block[:, dx * chans:(dx + 1) * chans]
-        return carry
-
-    lax.fori_loop(0, count, backward_step, 0)
+
+    def section(index):
+        if index == 0:
+            load_images.wait()
+        if index == segments - 1:
+            flip()
+            load_cotangent.wait()
+
+        def forward_step(n, carry):
+            forward(n, index)
+            if index == segments - 1:
+                backward(n, index)
+            turned_x[n] = spread_x[n, middle, chans:2 * chans].T
+            return carry
+
+        lax.fori_loop(0, count, forward_step, 0)
+        if index < segments - 1:
+            flip()
+        for k in range(1, replicas):
+            latent_copy(k, me).start()
+        acc[...] = jnp.zeros_like(acc)
+
+        def backward_step(n, carry):
+            if index < segments - 1:
+                backward(n, index)
+            add_weight_grad(n)
+            return carry
+
+        lax.fori_loop(0, count, backward_step, 0)
+
+        def finish(n, carry):
+            for piece in range(2):
+                if index < segments - 1:
+                    forward_copy(n, piece, cut_at(index), index + 1).wait_send()
+                if index > 0:
+                    backward_copy(
+                        n, piece, cut_at(segments - 1 - index), index - 1
+                    ).wait_send()
+            return carry
+
+        lax.fori_loop(0, count, finish, 0)
+
+    for index in range(segments):
+        pl.when(seg == index)(functools.partial(section, index))
 
     def acc_share(half, q):
         start = pl.multiple_of((half * chips + q) * share, share)
@@ -322,18 +353,6 @@
     for k in range(chips):
         relay_copy(k, 1 - core, lax.rem(chip + chips - k, chips)).wait_recv()
 
-    def finish(n, carry):
-        @pl.when(jnp.logical_not(last))
-        def _():
-            forward_copy(n).wait_send()
-
-        @pl.when(jnp.logical_not(first))
-        def _():
-            backward_copy(n).wait_send()
-
-        return carry
-
-    lax.fori_loop(0, count, finish, 0)
     for k in range(1, replicas):
         latent_copy(k, me).wait_send()
         rows_copy(k, me).wait_send()
@@ -345,6 +364,24 @@
         if k:
             chip_copy(k).wait_send()
             shard_copy(k, chip).wait_send()
+
+
+def results(
+    wgrad, weight, energy_grad, affine_in, bias_in, latent_in, weight_out, affine_out, bias_out,
+    latent_out,
+):
+    chans = weight.shape[1]
+    for start in range(0, weight.shape[0], chans):
+        block = slice(start, start + chans)
+        weight_out[block, :] = (
+            wgrad[block, :].astype(F32) + weight[block, :].astype(F32) * energy_grad[...]
+        )
+
+    @pl.when(pl.program_id(0) == 0)
+    def _():
+        affine_out[...] = affine_in[...]
+        bias_out[...] = bias_in[...]
+        latent_out[...] = latent_in[...]
 
 
 def body(images, latent, weight, affine, biases, cotangent):
@@ -393,7 +430,7 @@
             pltpu.VMEM((chips, share, chans), BF16), pltpu.VMEM((chips, share, chans), BF16),
             pltpu.VMEM((chips, share, chans), BF16), pltpu.VMEM((chips, share, chans), BF16),
             pltpu.VMEM((share, chans), F32),
-            dma((count,)), dma((count,)), dma((count,)), dma((count,)), dma((6,)),
+            dma((count, 2)), dma((count, 2)), dma((count, 2)), dma((count, 2)), dma((6,)),
             dma((replicas,)), dma((replicas,)), dma((replicas,)), dma((replicas,)),
             dma((segments,)), dma((segments,)),
             dma((chips,)), dma((chips,)), dma((chips,)), dma((chips,)),
@@ -406,8 +443,23 @@
         images.reshape(maps), latent, kernel.reshape(3, 3 * chans, chans), affine[0], biases,
         cotangent.reshape(maps),
     )
-    wgrad = wgrad.reshape(kernel.shape).astype(F32) + kernel.astype(F32) * energy_grad
-    return (wgrad[None], affine_grad[None], bias_grad, latent_grad)
+    def whole(array):
+        return pl.BlockSpec(array.shape, lambda step: (0, 0))
+
+    block = pl.BlockSpec((3 * chans, chans), lambda step: (step, 0))
+    small = (affine_grad, bias_grad, latent_grad)
+    weight_grad, affine_grad, bias_grad, latent_grad = pl.pallas_call(
+        results,
+        grid=(3,),
+        out_shape=(
+            jax.ShapeDtypeStruct((taps, chans), F32),
+            *[jax.ShapeDtypeStruct(array.shape, F32) for array in small],
+        ),
+        in_specs=[block, block, whole(energy_grad), *map(whole, small)],
+        out_specs=(block, *map(whole, small)),
+        compiler_params=pltpu.CompilerParams(vmem_limit_bytes=56 * 1024 * 1024),
+    )(wgrad.reshape(taps, chans), kernel.reshape(taps, chans), energy_grad, *small)
+    return (weight_grad.reshape(weight.shape), affine_grad[None], bias_grad, latent_grad)
 
 
 def solution(mesh):

time: 72.6 us -> 68.3 us (0.941)
  other arithmetic: 3.11 us -> 0 us
  local copies, waits for them, and re-layouts: 1.97 us -> 0 us
    pallas_call x0 -> x1, Pallas kernels: none -> 4.41 us  [body(): pl.pallas_call(results, grid=(3,), out_shape=(jax.ShapeDtypeStruct((taps,...]
    pallas_call x1, Pallas kernels: 66.7 us -> 63 us  [body(): pl.pallas_call(functools.partial(relay, segments, replicas, width), out_s...]
    add x1 -> x0, other arithmetic: 3.11 us -> none  [body(): wgrad.reshape(kernel.shape).astype(F32) + kernel.astype(F32) * energy_grad]
    unnamed x11 -> x0, local copies, waits for them, and re-layouts: 1.97 us -> none
where the time goes in v3:
time: 68.3 us; the launch traced here: 68.1 us
  Pallas kernels  67.4 us (99%)
    pallas_call x1, Pallas kernels, body(): pl.pallas_call(functools.partial(relay, segments, replicas, width), out_s...  63 us
    pallas_call x1, Pallas kernels, body(): pl.pallas_call(results, grid=(3,), out_shape=(jax.ShapeDtypeStruct((taps,...  4.41 us

profile of v3, /device:TPU:0, one launch (start us, length us, event | category | flops | bytes accessed | tf_op | source)
XLA Modules:
  0.0 68.1 jit_solution(16377178977847331630)
XLA Ops:
  0.6 63.0 %shard_map.93 = (bf16[2,4,288,256]{3,2,1,0:T(8,128)(2,1)}, f32[256,256]{1,0:T(8,128)}, f32[512,256]{1,0:T(8,128)}, f32[1,256]{1,0:T(1,128)}, f32[4,512]{1,0:T(4,128)}) custom-call(bf16[4,256,256]{2,1,0:T(8,128)(2,1)} %bitcast.11, f32[4,512]{1,0:T(4,128)} %latent.1, bf16[3,768,256]{2,1,0:T(8,128)(2,1)} %bitcast.8, f32[512,256]{1,0:T(8,128)} %bitcast.12, ...), custom_call_target="tpu_custom_call" | custom-call | tf_op jit(solution)/shard_map/pallas_call | solution.py:401
  63.7 4.4 %shard_map.94 = (f32[2304,256]{1,0:T(8,128)}, f32[512,256]{1,0:T(8,128)}, f32[1,256]{1,0:T(1,128)}, f32[4,512]{1,0:T(4,128)}) custom-call(bf16[2304,256]{1,0:T(8,128)(2,1)} %bitcast.10, bf16[2304,256]{1,0:T(8,128)(2,1)} %bitcast.9, f32[256,256]{1,0:T(8,128)} %get-tuple-element.14.energy_grad, f32[512,256]{1,0:T(8,128)} %get-tuple-element.15.affine_in, ...), custom_call_target="tpu_custom_call" | custom-call | tf_op jit(solution)/shard_map/pallas_call | solution.py:451

commit v4 on v3

--- a/solution.py
+++ b/solution.py
@@ -28,7 +28,7 @@
     images, latent, weight_in, affine_in, biases_in, cotangent,
     wgrad, energy_grad, affine_grad, bias_grad, latent_grad,
     fin, fout, gin, gout, weight, affine, biases, latents,
-    spread_x, turned_x, conv, slope, flipped, spread_g, acc, energy,
+    spread_x, turned_x, conv, slope, d_scaled, flipped, spread_g, acc, energy,
     styles, demod, d_demod, d_style, d_bias, rows, parts,
     pair_out, pair_in, chip_out, chip_in, own,
     f_send, f_recv, g_send, g_recv, loads, l_send, l_recv, r_send, r_recv, p_send, p_recv,
@@ -185,26 +185,36 @@
             conv[n, block, :] = convolved
             slope[n, block, :] = GAIN * (0.6 + 0.4 * gate + 0.4 * hidden * (1.0 - gate * gate))
 
+    def arrive(n, index, piece):
+        cut = cut_at(segments - 1 - index)
+        start, size = rows_of(cut + 1, piece)
+        block = slice(start, start + size)
+        if index < segments - 1:
+            backward_copy(n, piece, cut + 1, index + 1).wait_recv()
+        spread(
+            spread_g.at[n], gin[n, block, :].astype(F32) * (slope[n, block, :] * demod[n]), start
+        )
+
+    def push_back(n, index, piece):
+        cut = cut_at(segments - 1 - index)
+        start, size = rows_of(cut, piece)
+        out = slice(start, start + size)
+        back = conv3(spread_g.at[n], flipped, start, size)
+        if index > 0:
+            gout[n, out, :] = (back * styles[n]).astype(BF16)
+            backward_copy(n, piece, cut, index - 1).start()
+        d_scaled[n, out, :] = back
+
     def backward(n, index):
-        cut = cut_at(segments - 1 - index)
         for piece in range(2):
-            start, size = rows_of(cut + 1, piece)
-            block = slice(start, start + size)
-            if index < segments - 1:
-                backward_copy(n, piece, cut + 1, index + 1).wait_recv()
-            d_hidden = gin[n, block, :].astype(F32) * slope[n, block, :]
-            spread(spread_g.at[n], d_hidden * demod[n], start)
-            start, size = rows_of(cut, piece)
-            out = slice(start, start + size)
-            d_scaled = conv3(spread_g.at[n], flipped, start, size)
-            if index > 0:
-                gout[n, out, :] = (d_scaled * styles[n]).astype(BF16)
-                backward_copy(n, piece, cut, index - 1).start()
-            style_part = jnp.sum(d_scaled * fin[n, out, :].astype(F32), axis=0, keepdims=True)
-            demod_part = jnp.sum(d_hidden * conv[n, block, :], axis=0, keepdims=True)
-            d_style[n] = style_part if piece == 0 else d_style[n] + style_part
-            d_demod[n] = demod_part if piece == 0 else d_demod[n] + demod_part
-            d_bias[...] += jnp.sum(d_hidden, axis=0, keepdims=True)
+            arrive(n, index, piece)
+            push_back(n, index, piece)
+
+    def channel_sums(n):
+        d_hidden = gin[n].astype(F32) * slope[n]
+        d_bias[...] += jnp.sum(d_hidden, axis=0, keepdims=True)
+        d_demod[n] = jnp.sum(d_hidden * conv[n], axis=0, keepdims=True)
+        d_style[n] = jnp.sum(d_scaled[n] * fin[n].astype(F32), axis=0, keepdims=True)
 
     def add_weight_grad(n):
         for dy in range(3):
@@ -227,7 +237,6 @@
             forward(n, index)
             if index == segments - 1:
                 backward(n, index)
-            turned_x[n] = spread_x[n, middle, chans:2 * chans].T
             return carry
 
         lax.fori_loop(0, count, forward_step, 0)
@@ -237,13 +246,24 @@
             latent_copy(k, me).start()
         acc[...] = jnp.zeros_like(acc)
 
+        def turn(n, carry):
+            turned_x[n] = spread_x[n, middle, chans:2 * chans].T
+            return carry
+
+        lax.fori_loop(0, count, turn, 0)
+
         def backward_step(n, carry):
             if index < segments - 1:
                 backward(n, index)
+            channel_sums(n)
             add_weight_grad(n)
             return carry
 
-        lax.fori_loop(0, count, backward_step, 0)
+        lax.fori_loop(0, count - 1 if index == 0 else count, backward_step, 0)
+        if index == 0:
+            for piece in range(2):
+                arrive(count - 1, index, piece)
+            add_weight_grad(count - 1)
 
         def finish(n, carry):
             for piece in range(2):
@@ -288,6 +308,13 @@
     for k in order:
         pair_out[k] = acc_share(1 - core, lax.rem(chip + k, chips)).astype(BF16)
         pair_copy(k).start()
+
+    @pl.when(first)
+    def _():
+        for piece in range(2):
+            push_back(count - 1, 0, piece)
+        channel_sums(count - 1)
+
     for k in order:
         pair_copy(k).wait_recv()
         both = acc_share(core, lax.rem(chip + k, chips)) + pair_in[k].astype(F32)
@@ -368,20 +395,42 @@
 
 def results(
     wgrad, weight, energy_grad, affine_in, bias_in, latent_in, weight_out, affine_out, bias_out,
-    latent_out,
+    latent_out, wgrad_here, weight_here, energy_here, out_here, in_sems, out_sems, small_sems,
 ):
     chans = weight.shape[1]
-    for start in range(0, weight.shape[0], chans):
-        block = slice(start, start + chans)
-        weight_out[block, :] = (
-            wgrad[block, :].astype(F32) + weight[block, :].astype(F32) * energy_grad[...]
-        )
-
-    @pl.when(pl.program_id(0) == 0)
-    def _():
-        affine_out[...] = affine_in[...]
-        bias_out[...] = bias_in[...]
-        latent_out[...] = latent_in[...]
+    blocks = [pl.ds(start, chans) for start in range(0, weight.shape[0], chans)]
+    loads, stores = [], []
+    load_energy = pltpu.make_async_copy(energy_grad, energy_here, small_sems.at[0])
+    load_energy.start()
+    for tap, block in enumerate(blocks):
+        pair = (
+            pltpu.make_async_copy(wgrad.at[block], wgrad_here.at[block], in_sems.at[0, tap]),
+            pltpu.make_async_copy(weight.at[block], weight_here.at[block], in_sems.at[1, tap]),
+        )
+        for copy in pair:
+            copy.start()
+        loads.append(pair)
+    small = [
+        pltpu.make_async_copy(source, target, small_sems.at[place])
+        for place, (source, target) in enumerate(
+            ((affine_in, affine_out), (bias_in, bias_out), (latent_in, latent_out)), 1
+        )
+    ]
+    for copy in small:
+        copy.start()
+    load_energy.wait()
+    for tap, block in enumerate(blocks):
+        for copy in loads[tap]:
+            copy.wait()
+        out_here[block, :] = (
+            wgrad_here[block, :].astype(F32)
+            + weight_here[block, :].astype(F32) * energy_here[...]
+        )
+        store = pltpu.make_async_copy(out_here.at[block], weight_out.at[block], out_sems.at[tap])
+        store.start()
+        stores.append(store)
+    for copy in stores + small:
+        copy.wait()
 
 
 def body(images, latent, weight, affine, biases, cotangent):
@@ -418,7 +467,7 @@
             pltpu.VMEM((replicas,) + latent.shape, F32),
             pltpu.VMEM(tall, BF16),
             pltpu.VMEM((count, chans, pixels), BF16),
-            pltpu.VMEM(maps, F32), pltpu.VMEM(maps, F32),
+            pltpu.VMEM(maps, F32), pltpu.VMEM(maps, F32), pltpu.VMEM(maps, F32),
             pltpu.VMEM((3, 3 * chans, chans), BF16),
             pltpu.VMEM(tall, BF16),
             pltpu.VMEM((taps, chans), F32),
@@ -443,20 +492,20 @@
         images.reshape(maps), latent, kernel.reshape(3, 3 * chans, chans), affine[0], biases,
         cotangent.reshape(maps),
     )
-    def whole(array):
-        return pl.BlockSpec(array.shape, lambda step: (0, 0))
-
-    block = pl.BlockSpec((3 * chans, chans), lambda step: (step, 0))
     small = (affine_grad, bias_grad, latent_grad)
     weight_grad, affine_grad, bias_grad, latent_grad = pl.pallas_call(
         results,
-        grid=(3,),
         out_shape=(
             jax.ShapeDtypeStruct((taps, chans), F32),
             *[jax.ShapeDtypeStruct(array.shape, F32) for array in small],
         ),
-        in_specs=[block, block, whole(energy_grad), *map(whole, small)],
-        out_specs=(block, *map(whole, small)),
+        in_specs=[here] * 6,
+        out_specs=(here,) * 4,
+        scratch_shapes=[
+            pltpu.VMEM((taps, chans), BF16), pltpu.VMEM((taps, chans), BF16),
+            pltpu.VMEM((chans, chans), F32), pltpu.VMEM((taps, chans), F32),
+            dma((2, 9)), dma((9,)), dma((4,)),
+        ],
         compiler_params=pltpu.CompilerParams(vmem_limit_bytes=56 * 1024 * 1024),
     )(wgrad.reshape(taps, chans), kernel.reshape(taps, chans), energy_grad, *small)
     return (weight_grad.reshape(weight.shape), affine_grad[None], bias_grad, latent_grad)

time: 68.3 us -> 82.1 us (1.20)
  Pallas kernels: 67.4 us -> 81.1 us
    pallas_call x1, Pallas kernels: 4.41 us -> 17.6 us  [body(): pl.pallas_call(results, out_shape=(jax.ShapeDtypeStruct((taps, chans), F3...]
where the time goes in v4:
time: 82.1 us; the launch traced here: 81.9 us
  Pallas kernels  81.1 us (99%)
    pallas_call x1, Pallas kernels, body(): pl.pallas_call(functools.partial(relay, segments, replicas, width), out_s...  63.6 us
    pallas_call x1, Pallas kernels, body(): pl.pallas_call(results, out_shape=(jax.ShapeDtypeStruct((taps, chans), F3...  17.6 us

profile of v4, /device:TPU:0, one launch (start us, length us, event | category | flops | bytes accessed | tf_op | source)
XLA Modules:
  0.0 81.9 jit_solution(2111584437041483093)
XLA Ops:
  0.6 63.6 %shard_map.93 = (bf16[2,4,288,256]{3,2,1,0:T(8,128)(2,1)}, f32[256,256]{1,0:T(8,128)}, f32[512,256]{1,0:T(8,128)}, f32[1,256]{1,0:T(1,128)}, f32[4,512]{1,0:T(4,128)}) custom-call(bf16[4,256,256]{2,1,0:T(8,128)(2,1)} %bitcast.11, f32[4,512]{1,0:T(4,128)} %latent.1, bf16[3,768,256]{2,1,0:T(8,128)(2,1)} %bitcast.8, f32[512,256]{1,0:T(8,128)} %bitcast.12, ...), custom_call_target="tpu_custom_call" | custom-call | tf_op jit(solution)/shard_map/pallas_call | solution.py:450
  64.2 17.6 %shard_map.94 = (f32[2304,256]{1,0:T(8,128)}, f32[512,256]{1,0:T(8,128)}, f32[1,256]{1,0:T(1,128)}, f32[4,512]{1,0:T(4,128)}) custom-call(bf16[2304,256]{1,0:T(8,128)(2,1)} %bitcast.10, bf16[2304,256]{1,0:T(8,128)(2,1)} %bitcast.9, f32[256,256]{1,0:T(8,128)} %get-tuple-element.14.energy_grad, f32[512,256]{1,0:T(8,128)} %get-tuple-element.15.affine_in, ...), custom_call_target="tpu_custom_call" | custom-call | tf_op jit(solution)/shard_map/pallas_call | solution.py:496

commit v5 on v4

--- a/solution.py
+++ b/solution.py
@@ -229,28 +229,32 @@
     def section(index):
         if index == 0:
             load_images.wait()
+        if index > 0:
+            flip()
         if index == segments - 1:
-            flip()
             load_cotangent.wait()
+
+        def turn(n, carry):
+            turned_x[n] = spread_x[n, middle, chans:2 * chans].T
+            return carry
 
         def forward_step(n, carry):
             forward(n, index)
             if index == segments - 1:
                 backward(n, index)
+            elif index > 0:
+                turn(n, 0)
             return carry
 
         lax.fori_loop(0, count, forward_step, 0)
-        if index < segments - 1:
+        if index == 0:
             flip()
         for k in range(1, replicas):
             latent_copy(k, me).start()
         acc[...] = jnp.zeros_like(acc)
 
-        def turn(n, carry):
-            turned_x[n] = spread_x[n, middle, chans:2 * chans].T
-            return carry
-
-        lax.fori_loop(0, count, turn, 0)
+        if index in (0, segments - 1):
+            lax.fori_loop(0, count, turn, 0)
 
         def backward_step(n, carry):
             if index < segments - 1:
@@ -309,12 +313,6 @@
         pair_out[k] = acc_share(1 - core, lax.rem(chip + k, chips)).astype(BF16)
         pair_copy(k).start()
 
-    @pl.when(first)
-    def _():
-        for piece in range(2):
-            push_back(count - 1, 0, piece)
-        channel_sums(count - 1)
-
     for k in order:
         pair_copy(k).wait_recv()
         both = acc_share(core, lax.rem(chip + k, chips)) + pair_in[k].astype(F32)
@@ -323,6 +321,12 @@
             chip_copy(k).start()
         else:
             own[...] = both
+
+    @pl.when(first)
+    def _():
+        for piece in range(2):
+            push_back(count - 1, 0, piece)
+        channel_sums(count - 1)
 
     style_rows = jnp.concatenate([styles[n] for n in range(count)], axis=0)
     demod_rows = jnp.concatenate([demod[n] for n in range(count)], axis=0)
@@ -395,7 +399,8 @@
 
 def results(
     wgrad, weight, energy_grad, affine_in, bias_in, latent_in, weight_out, affine_out, bias_out,
-    latent_out, wgrad_here, weight_here, energy_here, out_here, in_sems, out_sems, small_sems,
+    latent_out, wgrad_here, weight_here, energy_here, out_here, affine_here, bias_here, latent_here,
+    in_sems, out_sems, small_sems,
 ):
     chans = weight.shape[1]
     blocks = [pl.ds(start, chans) for start in range(0, weight.shape[0], chans)]
@@ -410,14 +415,12 @@
         for copy in pair:
             copy.start()
         loads.append(pair)
-    small = [
-        pltpu.make_async_copy(source, target, small_sems.at[place])
-        for place, (source, target) in enumerate(
-            ((affine_in, affine_out), (bias_in, bias_out), (latent_in, latent_out)), 1
-        )
-    ]
-    for copy in small:
-        copy.start()
+    small = (
+        (affine_in, affine_here, affine_out), (bias_in, bias_here, bias_out),
+        (latent_in, latent_here, latent_out),
+    )
+    for place, (source, held, _) in enumerate(small):
+        pltpu.make_async_copy(source, held, small_sems.at[place + 1]).start()
     load_energy.wait()
     for tap, block in enumerate(blocks):
         for copy in loads[tap]:
@@ -429,7 +432,12 @@
         store = pltpu.make_async_copy(out_here.at[block], weight_out.at[block], out_sems.at[tap])
         store.start()
         stores.append(store)
-    for copy in stores + small:
+    for place, (source, held, target) in enumerate(small):
+        pltpu.make_async_copy(source, held, small_sems.at[place + 1]).wait()
+        store = pltpu.make_async_copy(held, target, out_sems.at[len(blocks) + place])
+        store.start()
+        stores.append(store)
+    for copy in stores:
         copy.wait()
 
 
@@ -504,7 +512,8 @@
         scratch_shapes=[
             pltpu.VMEM((taps, chans), BF16), pltpu.VMEM((taps, chans), BF16),
             pltpu.VMEM((chans, chans), F32), pltpu.VMEM((taps, chans), F32),
-            dma((2, 9)), dma((9,)), dma((4,)),
+            *[pltpu.VMEM(array.shape, F32) for array in small],
+            dma((2, 9)), dma((12,)), dma((4,)),
         ],
         compiler_params=pltpu.CompilerParams(vmem_limit_bytes=56 * 1024 * 1024),
     )(wgrad.reshape(taps, chans), kernel.reshape(taps, chans), energy_grad, *small)

time: 82.1 us -> 66.4 us (0.81)
  Pallas kernels: 81.1 us -> 65.6 us
    pallas_call x1, Pallas kernels: 17.6 us -> 3.52 us  [body(): pl.pallas_call(results, out_shape=(jax.ShapeDtypeStruct((taps, chans), F3...]
    pallas_call x1, Pallas kernels: 63.6 us -> 62.1 us  [body(): pl.pallas_call(functools.partial(relay, segments, replicas, width), out_s...]
where the time goes in v5:
time: 66.4 us; the launch traced here: 66.3 us
  Pallas kernels  65.6 us (99%)
    pallas_call x1, Pallas kernels, body(): pl.pallas_call(functools.partial(relay, segments, replicas, width), out_s...  62.1 us
    pallas_call x1, Pallas kernels, body(): pl.pallas_call(results, out_shape=(jax.ShapeDtypeStruct((taps, chans), F3...  3.52 us

profile of v5, /device:TPU:0, one launch (start us, length us, event | category | flops | bytes accessed | tf_op | source)
XLA Modules:
  0.0 66.3 jit_solution(18152296117671043149)
XLA Ops:
  0.6 62.1 %shard_map.93 = (bf16[2,4,288,256]{3,2,1,0:T(8,128)(2,1)}, f32[256,256]{1,0:T(8,128)}, f32[512,256]{1,0:T(8,128)}, f32[1,256]{1,0:T(1,128)}, f32[4,512]{1,0:T(4,128)}) custom-call(bf16[4,256,256]{2,1,0:T(8,128)(2,1)} %bitcast.11, f32[4,512]{1,0:T(4,128)} %latent.1, bf16[3,768,256]{2,1,0:T(8,128)(2,1)} %bitcast.8, f32[512,256]{1,0:T(8,128)} %bitcast.12, ...), custom_call_target="tpu_custom_call" | custom-call | tf_op jit(solution)/shard_map/pallas_call | solution.py:458
  62.8 3.5 %shard_map.94 = (f32[2304,256]{1,0:T(8,128)}, f32[512,256]{1,0:T(8,128)}, f32[1,256]{1,0:T(1,128)}, f32[4,512]{1,0:T(4,128)}) custom-call(bf16[2304,256]{1,0:T(8,128)(2,1)} %bitcast.10, bf16[2304,256]{1,0:T(8,128)(2,1)} %bitcast.9, f32[256,256]{1,0:T(8,128)} %get-tuple-element.14.energy_grad, f32[512,256]{1,0:T(8,128)} %get-tuple-element.15.affine_in, ...), custom_call_target="tpu_custom_call" | custom-call | tf_op jit(solution)/shard_map/pallas_call | solution.py:504

commit v6 on v5

--- a/solution.py
+++ b/solution.py
@@ -165,6 +165,9 @@
 
     pl.semaphore_wait(barrier, replicas + segments - 2)
 
+    def slope_of(hidden, gate):
+        return GAIN * (0.6 + 0.4 * gate + 0.4 * hidden * (1.0 - gate * gate))
+
     def forward(n, index):
         cut = cut_at(index)
         for piece in range(2):
@@ -183,7 +186,8 @@
                 fout[n, block, :] = (GAIN * hidden * (0.6 + 0.4 * gate)).astype(BF16)
                 forward_copy(n, piece, cut, index + 1).start()
             conv[n, block, :] = convolved
-            slope[n, block, :] = GAIN * (0.6 + 0.4 * gate + 0.4 * hidden * (1.0 - gate * gate))
+            if index > 0:
+                slope[n, block, :] = slope_of(hidden, gate)
 
     def arrive(n, index, piece):
         cut = cut_at(segments - 1 - index)
@@ -249,6 +253,13 @@
         lax.fori_loop(0, count, forward_step, 0)
         if index == 0:
             flip()
+
+            def steepen(n, carry):
+                hidden = conv[n] * demod[n] + biases[...]
+                slope[n] = slope_of(hidden, jnp.tanh(hidden))
+                return carry
+
+            lax.fori_loop(0, count, steepen, 0)
         for k in range(1, replicas):
             latent_copy(k, me).start()
         acc[...] = jnp.zeros_like(acc)

time: 66.4 us -> 66.4 us (level)
  no operation moved by 1% of the time
where the time goes in v6:
time: 66.4 us; the launch traced here: 66.2 us
  Pallas kernels  65.6 us (99%)
    pallas_call x1, Pallas kernels, body(): pl.pallas_call(functools.partial(relay, segments, replicas, width), out_s...  62.1 us
    pallas_call x1, Pallas kernels, body(): pl.pallas_call(results, out_shape=(jax.ShapeDtypeStruct((taps, chans), F3...  3.52 us

profile of v6, /device:TPU:0, one launch (start us, length us, event | category | flops | bytes accessed | tf_op | source)
XLA Modules:
  0.0 66.2 jit_solution(10466260882301076337)
XLA Ops:
  0.6 62.1 %shard_map.93 = (bf16[2,4,288,256]{3,2,1,0:T(8,128)(2,1)}, f32[256,256]{1,0:T(8,128)}, f32[512,256]{1,0:T(8,128)}, f32[1,256]{1,0:T(1,128)}, f32[4,512]{1,0:T(4,128)}) custom-call(bf16[4,256,256]{2,1,0:T(8,128)(2,1)} %bitcast.11, f32[4,512]{1,0:T(4,128)} %latent.1, bf16[3,768,256]{2,1,0:T(8,128)(2,1)} %bitcast.8, f32[512,256]{1,0:T(8,128)} %bitcast.12, ...), custom_call_target="tpu_custom_call" | custom-call | tf_op jit(solution)/shard_map/pallas_call | solution.py:469
  62.7 3.5 %shard_map.94 = (f32[2304,256]{1,0:T(8,128)}, f32[512,256]{1,0:T(8,128)}, f32[1,256]{1,0:T(1,128)}, f32[4,512]{1,0:T(4,128)}) custom-call(bf16[2304,256]{1,0:T(8,128)(2,1)} %bitcast.10, bf16[2304,256]{1,0:T(8,128)(2,1)} %bitcast.9, f32[256,256]{1,0:T(8,128)} %get-tuple-element.14.energy_grad, f32[512,256]{1,0:T(8,128)} %get-tuple-element.15.affine_in, ...), custom_call_target="tpu_custom_call" | custom-call | tf_op jit(solution)/shard_map/pallas_call | solution.py:515
